TPU v7x, 32 devices: a whole 2x2x4 slice. The times are simulated.
32 devices in a mesh: fsdp: 8 (over z, y), heads: 4 (over x, core).
Axes of the slice: x: 2, y: 2, z: 4, core: 2. Of those that a mesh axis runs over, the one named last changes fastest.
Arguments:
- activations: bfloat16 [1024, 2048], P('fsdp'), may hold values from -6 to 6
- norm_gains: bfloat16 [2, 2048], P(None, 'fsdp'), may hold values from 0.099609375 to 1.8984375
- w_query: bfloat16 [2048, 4, 512], P('fsdp', 'heads'), may hold values from -0.125 to 0.125
- w_keyval: bfloat16 [2048, 4, 128], P('fsdp', 'heads'), may hold values from -0.125 to 0.125
- w_out: bfloat16 [4, 512, 2048], P('heads', None, 'fsdp'), may hold values from -0.375 to 0.375
- w_gateup: bfloat16 [2048, 2, 5632], P('fsdp', None, 'heads'), may hold values from -0.125 to 0.125
- w_down: bfloat16 [5632, 2048], P('heads', 'fsdp'), may hold values from -0.078125 to 0.078125
- seq_lengths: int32 [3], replicated, may hold values from 1 to 512, 1024 in all
- token_slot: int32 [1024], P('fsdp'), may hold values from 0 to 1023, as said below
- out_grad: bfloat16 [1024, 2048], P('fsdp'), may hold values from -6 to 6
Outputs:
- block_out: bfloat16 [1024, 2048], P('fsdp')
- input_grad: float32 [1024, 2048], P('fsdp')
- grad_gains: float32 [2, 2048], P(None, 'fsdp')
- grad_query: float32 [2048, 4, 512], P('fsdp', 'heads')
- grad_keyval: float32 [2048, 4, 128], P('fsdp', 'heads')
- grad_out: float32 [4, 512, 2048], P('heads', None, 'fsdp')
- grad_gateup: float32 [2048, 2, 5632], P('fsdp', None, 'heads')
- grad_down: float32 [5632, 2048], P('heads', 'fsdp')
Inputs may be any that keep to these rules, and one draw needn't show every extreme that they name: `seq_lengths`: the lengths sum to 1024; the longest is exactly 512. `token_slot`: A permutation of the pack's places. Each device of fsdp holds exactly one place of every aligned block of 8 consecutive places, and its places rise with the row.
All inputs are finite; a program needn't handle non-finite values.
Results may differ from a plain program's by a relative error of at most 0.02.
Values may be sent and summed in bfloat16 or wider, within the bound.
No kernel may reach another device: no remote copies, remote signals or barrier semaphores. Data moves between devices by JAX's collectives and lax.ppermute only.
A program may use at most 128 MiB of HBM per device.

v0:
```python
import jax
import jax.numpy as jnp
from jax import lax
from jax.sharding import PartitionSpec as P

HD = 64


epsilon = 1e-05
rope_base = 10000.0
masked_fill = -1e30


def cut_along(x, dim, devices):
    before, after = (x.shape[:dim], x.shape[dim + 1 :])
    return jnp.moveaxis(x.reshape(*before, devices, -1, *after), dim, 0)


def sent_and_summed(x, axis, dim):
    devices = lax.axis_size(axis)
    pieces = lax.all_to_all(cut_along(x, dim, devices), axis, 0, 0, tiled=True)
    return jnp.sum(pieces.astype(jnp.float32), axis=0)


def locate(seq_lengths, slot_values):
    seq_ends = jnp.cumsum(seq_lengths)
    seq_starts = seq_ends - seq_lengths
    inside = (slot_values[:, None] >= seq_starts[None, :]) & (
        slot_values[:, None] < seq_ends[None, :]
    )
    first_slot = jnp.sum(jnp.where(inside, seq_starts[None, :], 0), axis=1)
    return (first_slot, slot_values - first_slot)


def rotation(position):
    half_width = HD // 2
    frequency = rope_base ** (-jnp.arange(half_width, dtype=jnp.float32) * 2.0 / HD)
    angles = position.astype(jnp.float32)[:, None] * frequency[None, :]
    return (jnp.cos(angles), jnp.sin(angles))


def rotate(values, cosine_table, sine_table):
    half_width = values.shape[-1] // 2
    table_shape = (cosine_table.shape[0],) + (1,) * (values.ndim - 2) + (half_width,)
    cosine_part = cosine_table.reshape(table_shape)
    sine_part = sine_table.reshape(table_shape)
    first_half = values[..., :half_width]
    second_half = values[..., half_width:]
    return jnp.concatenate(
        [
            first_half * cosine_part - second_half * sine_part,
            second_half * cosine_part + first_half * sine_part,
        ],
        axis=-1,
    )


def normalize(values):
    return values * lax.rsqrt(jnp.mean(values * values, axis=-1, keepdims=True) + epsilon)


def norm_back(values, normed, incoming):
    scale = lax.rsqrt(jnp.mean(values * values, axis=-1, keepdims=True) + epsilon)
    return scale * (incoming - normed * jnp.mean(incoming * normed, axis=-1, keepdims=True))


def divisor_rows(total_rows, row_limit):
    for candidate in range(min(total_rows, row_limit), 0, -1):
        if total_rows % candidate == 0:
            return candidate
    return 1


def on_device(
    activations,
    norm_gains,
    w_query,
    w_keyval,
    w_out,
    w_gateup,
    w_down,
    seq_lengths,
    token_slot,
    out_grad,
):
    tok_rows = activations.shape[0]
    local_heads = w_query.shape[1]
    groups = w_query.shape[2] // HD
    first_slot, position = locate(seq_lengths, token_slot)
    cosine_table, sine_table = rotation(position)
    query_w, keyval_w, out_w, gains_full = (
        lax.all_gather(w_query, "fsdp", axis=0, tiled=True),
        lax.all_gather(w_keyval, "fsdp", axis=0, tiled=True),
        lax.all_gather(w_out, "fsdp", axis=2, tiled=True),
        lax.all_gather(norm_gains, "fsdp", axis=1, tiled=True),
    )
    gains = gains_full.astype(jnp.float32)
    inputs = activations.astype(jnp.float32)
    normed_one = normalize(inputs)
    lowered_one = (normed_one * gains[0]).astype(jnp.bfloat16)
    query_lin = jnp.einsum("td,dhe->the", lowered_one, query_w, preferred_element_type=jnp.float32)
    keyval_lin = jnp.einsum(
        "td,dhe->the", lowered_one, keyval_w, preferred_element_type=jnp.float32
    )
    queries = rotate(
        query_lin.reshape(tok_rows, local_heads, groups, HD), cosine_table, sine_table
    ).astype(jnp.bfloat16)
    key_rows = rotate(keyval_lin[..., :HD], cosine_table, sine_table).astype(jnp.bfloat16)
    keyvals = jnp.concatenate([key_rows, keyval_lin[..., HD:].astype(jnp.bfloat16)], axis=-1)
    slot_column = token_slot[:, None]
    first_column = first_slot[:, None]

    def scores_of(key_block, slot_block):
        logits = (
            jnp.einsum("tgqd,kgd->tgqk", queries, key_block, preferred_element_type=jnp.float32)
            * 0.125
        )
        allowed = (slot_block[None, :] <= slot_column) & (slot_block[None, :] >= first_column)
        return (logits, allowed[:, None, None, :])

    def absorb(running, blocks):
        running_max, running_sum, running_out = running
        key_block, slot_block = blocks
        logits, allowed = scores_of(key_block[..., :HD], slot_block)
        newest = jnp.maximum(running_max, jnp.max(jnp.where(allowed, logits, masked_fill), axis=-1))
        weights = jnp.where(allowed, jnp.exp(logits - newest[..., None]), 0.0)
        factor = jnp.exp(running_max - newest)
        running_sum = running_sum * factor + jnp.sum(weights, axis=-1)
        running_out = running_out * factor[..., None] + jnp.einsum(
            "tgqk,kgd->tgqd",
            weights.astype(jnp.bfloat16),
            key_block[..., HD:],
            preferred_element_type=jnp.float32,
        )
        return ((newest, running_sum, running_out), None)

    start_state = (
        jnp.full((tok_rows, local_heads, groups), masked_fill, jnp.float32),
        jnp.zeros((tok_rows, local_heads, groups), jnp.float32),
        jnp.zeros((tok_rows, local_heads, groups, HD), jnp.float32),
    )
    running = start_state
    key_piece = lax.all_gather(keyvals, "fsdp", axis=0, tiled=True)
    slot_piece = lax.all_gather(token_slot, "fsdp", axis=0, tiled=True)
    piece_rows = key_piece.shape[0]
    block_rows = divisor_rows(piece_rows, 512)
    blocks = (
        key_piece.reshape(piece_rows // block_rows, block_rows, local_heads, 2 * HD),
        slot_piece.reshape(piece_rows // block_rows, block_rows),
    )
    running, unused = lax.scan(absorb, running, blocks)
    final_max, final_sum, final_out = running
    attended = final_out / final_sum[..., None]
    log_total = final_max + jnp.log(final_sum)
    attended_low = attended.reshape(tok_rows, local_heads, groups * HD).astype(jnp.bfloat16)
    branch_part = jnp.einsum("the,hed->td", attended_low, out_w, preferred_element_type=jnp.float32)
    branch = lax.psum(branch_part.astype(jnp.bfloat16), "heads").astype(jnp.float32)
    middle = inputs + branch
    normed_two = normalize(middle)
    lowered_two = (normed_two * gains[1]).astype(jnp.bfloat16)
    gateup_w, down_w = (
        lax.all_gather(w_gateup, "fsdp", axis=0, tiled=True),
        lax.all_gather(w_down, "fsdp", axis=1, tiled=True),
    )
    gateup = jnp.einsum("td,dce->tce", lowered_two, gateup_w, preferred_element_type=jnp.float32)
    gate_pre = gateup[:, 0]
    up_pre = gateup[:, 1]
    sigmoid_gate = jax.nn.sigmoid(gate_pre)
    activated = gate_pre * sigmoid_gate
    hidden = (activated * up_pre).astype(jnp.bfloat16)
    mixed_part = jnp.dot(hidden, down_w, preferred_element_type=jnp.float32)
    mixed = lax.psum(mixed_part.astype(jnp.bfloat16), "heads").astype(jnp.float32)
    block_out = (middle + mixed).astype(jnp.bfloat16)
    gateup_back, down_back = (
        lax.all_gather(w_gateup, "fsdp", axis=0, tiled=True),
        lax.all_gather(w_down, "fsdp", axis=1, tiled=True),
    )
    upstream = out_grad.astype(jnp.float32)
    hidden_grad = jnp.einsum("td,fd->tf", out_grad, down_back, preferred_element_type=jnp.float32)
    gate_grad = hidden_grad * up_pre * sigmoid_gate * (1.0 + gate_pre * (1.0 - sigmoid_gate))
    up_grad = hidden_grad * activated
    gateup_grad = jnp.stack([gate_grad, up_grad], axis=1).astype(jnp.bfloat16)
    down_term = jnp.einsum("tf,td->fd", hidden, out_grad, preferred_element_type=jnp.float32)
    gateup_term = jnp.einsum(
        "td,tce->dce", lowered_two, gateup_grad, preferred_element_type=jnp.float32
    )
    lowered_grad_two = lax.psum(
        jnp.einsum(
            "tce,dce->td", gateup_grad, gateup_back, preferred_element_type=jnp.float32
        ).astype(jnp.bfloat16),
        "heads",
    ).astype(jnp.float32)
    gain_grad_two = jnp.sum(lowered_grad_two * normed_two, axis=0)
    middle_grad = upstream + norm_back(middle, normed_two, lowered_grad_two * gains[1])
    gateup_owned, down_owned = (
        lax.psum_scatter(gateup_term, "fsdp", scatter_dimension=0, tiled=True),
        lax.psum_scatter(down_term, "fsdp", scatter_dimension=1, tiled=True),
    )
    branch_grad = middle_grad.astype(jnp.bfloat16)
    out_term = jnp.einsum(
        "the,td->hed", attended_low, branch_grad, preferred_element_type=jnp.float32
    )
    query_back, keyval_back, out_back = (
        lax.all_gather(w_query, "fsdp", axis=0, tiled=True),
        lax.all_gather(w_keyval, "fsdp", axis=0, tiled=True),
        lax.all_gather(w_out, "fsdp", axis=2, tiled=True),
    )
    attended_grad = jnp.einsum(
        "td,hed->the", branch_grad, out_back, preferred_element_type=jnp.float32
    )
    attended_grad = attended_grad.reshape(tok_rows, local_heads, groups, HD).astype(jnp.bfloat16)
    delta = jnp.sum(attended_grad.astype(jnp.float32) * attended, axis=-1)
    key_all, slot_all = (
        lax.all_gather(keyvals, "fsdp", axis=0, tiled=True),
        lax.all_gather(token_slot, "fsdp", axis=0, tiled=True),
    )
    total_keys = key_all.shape[0]
    block_rows = divisor_rows(total_keys, 512)

    def backstep(query_grad, blocks):
        key_block, slot_block = blocks
        logits, allowed = scores_of(key_block[..., :HD], slot_block)
        probs = jnp.where(allowed, jnp.exp(logits - log_total[..., None]), 0.0)
        value_grad = jnp.einsum(
            "tgqk,tgqd->kgd",
            probs.astype(jnp.bfloat16),
            attended_grad,
            preferred_element_type=jnp.float32,
        )
        prob_grad = jnp.einsum(
            "tgqd,kgd->tgqk", attended_grad, key_block[..., HD:], preferred_element_type=jnp.float32
        )
        score_grad = (probs * (prob_grad - delta[..., None])).astype(jnp.bfloat16)
        query_grad = query_grad + 0.125 * jnp.einsum(
            "tgqk,kgd->tgqd", score_grad, key_block[..., :HD], preferred_element_type=jnp.float32
        )
        key_grad = 0.125 * jnp.einsum(
            "tgqk,tgqd->kgd", score_grad, queries, preferred_element_type=jnp.float32
        )
        return (query_grad, jnp.concatenate([key_grad, value_grad], axis=-1))

    key_blocks = (
        key_all.reshape(total_keys // block_rows, block_rows, local_heads, 2 * HD),
        slot_all.reshape(total_keys // block_rows, block_rows),
    )
    query_grad, keyval_terms = lax.scan(
        backstep, jnp.zeros((tok_rows, local_heads, groups, HD), jnp.float32), key_blocks
    )
    keyval_terms = keyval_terms.reshape(total_keys, local_heads, 2 * HD)
    keyval_sum = sent_and_summed(keyval_terms.astype(jnp.bfloat16), "fsdp", 0)
    key_unrotated = rotate(keyval_sum[..., :HD], cosine_table, -sine_table)
    keyval_grad = jnp.concatenate([key_unrotated, keyval_sum[..., HD:]], axis=-1).astype(
        jnp.bfloat16
    )
    query_lin_grad = (
        rotate(query_grad, cosine_table, -sine_table)
        .reshape(tok_rows, local_heads, groups * HD)
        .astype(jnp.bfloat16)
    )
    query_term = jnp.einsum(
        "td,the->dhe", lowered_one, query_lin_grad, preferred_element_type=jnp.float32
    )
    keyval_term = jnp.einsum(
        "td,the->dhe", lowered_one, keyval_grad, preferred_element_type=jnp.float32
    )
    lowered_part = jnp.einsum(
        "the,dhe->td", query_lin_grad, query_back, preferred_element_type=jnp.float32
    ) + jnp.einsum("the,dhe->td", keyval_grad, keyval_back, preferred_element_type=jnp.float32)
    lowered_grad_one = lax.psum(lowered_part.astype(jnp.bfloat16), "heads").astype(jnp.float32)
    gain_grad_one = jnp.sum(lowered_grad_one * normed_one, axis=0)
    input_grad = middle_grad + norm_back(inputs, normed_one, lowered_grad_one * gains[0])
    gain_terms = jnp.stack([gain_grad_one, gain_grad_two], axis=0)
    query_owned, keyval_owned, out_owned, gains_owned = (
        lax.psum_scatter(query_term, "fsdp", scatter_dimension=0, tiled=True),
        lax.psum_scatter(keyval_term, "fsdp", scatter_dimension=0, tiled=True),
        lax.psum_scatter(out_term, "fsdp", scatter_dimension=2, tiled=True),
        lax.psum_scatter(gain_terms, "fsdp", scatter_dimension=1, tiled=True),
    )
    return (
        block_out,
        input_grad,
        gains_owned,
        query_owned,
        keyval_owned,
        out_owned,
        gateup_owned,
        down_owned,
    )


def solution(mesh):
    placed = (
        P("fsdp", None),
        P(None, "fsdp"),
        P("fsdp", "heads", None),
        P("fsdp", "heads", None),
        P("heads", None, "fsdp"),
        P("fsdp", None, "heads"),
        P("heads", "fsdp"),
        P(),
        P("fsdp"),
        P("fsdp", None),
    )
    return jax.shard_map(
        on_device,
        mesh=mesh,
        in_specs=placed,
        out_specs=(
            P("fsdp", None),
            P("fsdp", None),
            P(None, "fsdp"),
            P("fsdp", "heads", None),
            P("fsdp", "heads", None),
            P("heads", None, "fsdp"),
            P("fsdp", None, "heads"),
            P("heads", "fsdp"),
        ),
        check_vma=False,
    )
```

profile of v0, /device:TPU:0, one launch (start us, length us, event | category | flops | bytes accessed | tf_op | source)
XLA Modules:
  0.0 1439.4 jit_solution(7148420679714297060)
XLA Ops:
  10.2 34.0 %all_gather.33 = bf16[2048,1,128]{2,0,1:T(8,128)(2,1)S(1)} all-gather(bf16[256,1,128]{2,0,1:T(8,128)(2,1)} %param.17), channel_id=1, replica_groups=mesh['fsdp'=8,'heads'=4] {'fsdp'}, dimensions={0}, use_global_device_ids=true | all-gather | bytes 589824 | tf_op jit(solution)/shard_map/all_gather | solution.py:93
  44.2 21.1 %all_gather.32 = bf16[2,2048]{1,0:T(2,128)(2,1)S(1)} all-gather(bf16[2,256]{1,0:T(2,128)(2,1)} %param.15), channel_id=1, replica_groups=mesh['fsdp'=8,'heads'=4] {'fsdp'}, dimensions={1}, use_global_device_ids=true | all-gather | bytes 9216 | tf_op jit(solution)/shard_map/all_gather | solution.py:95
  70.9 16.6 %all-gather = s32[8,1,128]{2,1,0:T(1,128)S(1)} all-gather(s32[1,1,128]{2,1,0:T(1,128)} %bitcast), channel_id=1, replica_groups=mesh['fsdp'=8,'heads'=4] {'fsdp'}, dimensions={0}, use_global_device_ids=true | all-gather | bytes 4608 | tf_op jit(solution)/shard_map/all_gather | solution.py:144
  89.2 27.7 %all_gather.34 = bf16[1024,1,128]{0,2,1:T(8,128)(2,1)S(1)} all-gather(bf16[128,1,128]{0,2,1:T(8,128)(2,1)S(1)} %pad_maximum_fusion.4), channel_id=1, replica_groups=mesh['fsdp'=8,'heads'=4] {'fsdp'}, dimensions={0}, use_global_device_ids=true | all-gather | bytes 294912 | tf_op jit(solution)/shard_map/all_gather | solution.py:143
  121.5 7.9 while.28
  135.3 28.3 %all-reduce.5.cloned.1.call-done = bf16[128,2048]{1,0:T(8,128)(2,1)} async-done(((bf16[128,2048]{1,0:T(8,128)(2,1)}), bf16[128,2048]{1,0:T(8,128)(2,1)}) %all-reduce.5.cloned.1.call-update) | async-done | bytes 524304 | tf_op jit(solution)/shard_map/psum | solution.py:157
  164.9 165.0 %all-gather.10.cloned.1.call-done = bf16[2048,2,1408]{2,0,1:T(8,128)(2,1)} async-done(((bf16[256,2,1408]{2,0,1:T(8,128)(2,1)}), bf16[2048,2,1408]{2,0,1:T(8,128)(2,1)}) %all-gather.10.cloned.1.call-update) | async-done | bytes 11534352 | tf_op jit(solution)/shard_map/all_gather | solution.py:162
  329.9 6.2 fusion.92
  336.1 87.5 %all-gather.12.cloned.1.call-done = bf16[1408,2048]{1,0:T(8,128)(2,1)} async-done(((bf16[1408,256]{1,0:T(8,128)(2,1)}), bf16[1408,2048]{1,0:T(8,128)(2,1)}) %all-gather.12.cloned.1.call-update) | async-done | bytes 5767184 | tf_op jit(solution)/shard_map/all_gather | solution.py:163
  423.6 4.6 fusion.62
  429.1 8.9 fusion.30
  442.5 27.0 %all-reduce.7.cloned.1.call-done = bf16[128,2048]{1,0:T(8,128)(2,1)} async-done(((bf16[128,2048]{1,0:T(8,128)(2,1)}), bf16[128,2048]{1,0:T(8,128)(2,1)}) %all-reduce.7.cloned.1.call-update) | async-done | bytes 524304 | tf_op jit(solution)/shard_map/psum | solution.py:187
  475.0 16.1 %while.29 = (s32[]{:T(128)}, f32[128,1,8,64]{0,3,2,1:T(8,128)}, bf16[2,512,1,128]{3,1,0,2:T(8,128)(2,1)}, bf16[2,512,1,128]{1,3,2,0:T(8,128)(2,1)}, s32[2,512]{1...) while((s32[]{:T(128)}, f32[128,1,8,64]{0,3,2,1:T(8,128)}, ...), condition=%wide.region_14.15_spmd.clone, body=%wide.region_13.14_spmd.clone.sunk | while | flops 339935232 | bytes 12008603 | solution.py:246
  491.0 5.5 all-to-all-start
  506.3 34.2 %all-reduce.9.cloned.1.call-done = (bf16[128,2048]{1,0:T(8,128)(2,1)}, bf16[128,2048]{1,0:T(8,128)(2,1)}) async-done(((bf16[128,2048]{1,0:T(8,128)(2,1)}, bf16[128,2048]{1,0:T(8,128)(2,1)}), (bf16[128,2048]{1,0:T(8,128)(2,1)}, bf16[128,2048]{1,0:T(8,128)(2,1)})) %all-reduce.9.cloned.1.call-update) | async-done | bytes 1048592 | tf_op jit(solution)/shard_map/psum | solution.py:172
  547.5 9.7 fusion.60
  562.5 5.9 fusion.101
  571.6 37.2 %reduce-scatter.19.cloned.1.call-done = f32[256,2]{1,0:T(8,128)} async-done(((f32[2048,2]{1,0:T(8,128)}), f32[256,2]{1,0:T(8,128)}) %reduce-scatter.19.cloned.1.call-update) | async-done | bytes 2064
  610.3 89.1 %reduce-scatter.9.cloned.1.call-done = f32[256,1,512]{2,0,1:T(8,128)} async-done(((f32[2048,1,512]{2,0,1:T(8,128)}), f32[256,1,512]{2,0,1:T(8,128)}) %reduce-scatter.9.cloned.1.call-update) | async-done | bytes 524304 | tf_op jit(solution)/shard_map/reduce_scatter | solution.py:274
  701.8 375.2 %reduce-scatter.15.cloned.1.call-done = f32[256,2,1408]{2,0,1:T(8,128)} async-done(((f32[2048,2,1408]{2,0,1:T(8,128)}), f32[256,2,1408]{2,0,1:T(8,128)}) %reduce-scatter.15.cloned.1.call-update) | async-done | bytes 2883600 | tf_op jit(solution)/shard_map/reduce_scatter | solution.py:196
  1077.0 5.6 copy.74
  1082.6 61.4 %reduce-scatter.11.cloned.1.call-done = f32[256,1,128]{2,0,1:T(8,128)} async-done(((f32[2048,1,128]{2,0,1:T(8,128)}), f32[256,1,128]{2,0,1:T(8,128)}) %reduce-scatter.11.cloned.1.call-update) | async-done | bytes 131088 | tf_op jit(solution)/shard_map/reduce_scatter | solution.py:275
  1144.1 91.4 %reduce-scatter.13.cloned.1.call-done = f32[1,512,256]{2,1,0:T(8,128)} async-done(((f32[1,512,2048]{2,1,0:T(8,128)}), f32[1,512,256]{2,1,0:T(8,128)}) %reduce-scatter.13.cloned.1.call-update) | async-done | bytes 524304 | tf_op jit(solution)/shard_map/reduce_scatter | solution.py:276
  1235.4 197.5 %reduce-scatter.17.cloned.1.call-done = f32[1408,256]{1,0:T(8,128)} async-done(((f32[1408,2048]{1,0:T(8,128)}), f32[1408,256]{1,0:T(8,128)}) %reduce-scatter.17.cloned.1.call-update) | async-done | bytes 1441808 | tf_op jit(solution)/shard_map/reduce_scatter | solution.py:197
  (187 shorter events, 85.3 us)
Async XLA Ops:
  7.2 110.5 %all-gather.6.cloned.1.call-start = ((), (), s32[]{:S(2)}) async-start(), calls=%async_computation.7 | async-start | bytes 2359296 | tf_op jit(solution)/shard_map/all_gather | solution.py:92
  7.9 121.6 %all-gather.8.cloned.1.call-start = ((), (), s32[]{:S(2)}) async-start(), calls=%async_computation.8 | async-start | bytes 2359296 | tf_op jit(solution)/shard_map/all_gather | solution.py:94
  8.6 154.9 %all-reduce.5.cloned.1.call-start = ((), (), s32[]{:S(2)}) async-start(), calls=%async_computation.9 | async-start | bytes 1048576 | tf_op jit(solution)/shard_map/psum | solution.py:157
  8.7 78.7 %copy-start.26 = (f32[32]{0:T(128)}, f32[32]{0:T(128)S(1)}, u32[]{:S(2)}) copy-start(f32[32]{0:T(128)S(1)} %multiply_power_fusion) | copy-start | bytes 388
  44.2 22.3 %copy-start.8 = (bf16[2048,1,128]{2,0,1:T(8,128)(2,1)}, bf16[2048,1,128]{2,0,1:T(8,128)(2,1)S(1)}, u32[]{:S(2)}) copy-start(bf16[2048,1,128]{2,0,1:T(8,128)(2,1)S(1)} %all_gather.33) | copy-start | bytes 1572868
  66.6 54.1 %copy-start.24 = (f32[128]{0:T(128)}, f32[128]{0:T(128)S(1)}, u32[]{:S(2)}) copy-start(f32[128]{0:T(128)S(1)} %add_rsqrt_fusion.1) | copy-start | bytes 1540
  70.9 50.6 %copy-start.20 = (f32[128,32]{0,1:T(8,128)}, f32[128,32]{0,1:T(8,128)S(1)}, u32[]{:S(2)}) copy-start(f32[128,32]{0,1:T(8,128)S(1)} %get-tuple-element.365) | copy-start | bytes 49156
  132.5 197.3 %all-gather.10.cloned.1.call-start = ((), (), s32[]{:S(2)}) async-start(), calls=%async_computation.10 | async-start | bytes 12976128 | tf_op jit(solution)/shard_map/all_gather | solution.py:162
  133.8 289.7 %all-gather.12.cloned.1.call-start = ((), (), s32[]{:S(2)}) async-start(), calls=%async_computation.11 | async-start | bytes 6488064 | tf_op jit(solution)/shard_map/all_gather | solution.py:163
  134.4 335.1 %all-reduce.7.cloned.1.call-start = ((), (), s32[]{:S(2)}) async-start(), calls=%async_computation.12 | async-start | bytes 1048576 | tf_op jit(solution)/shard_map/psum | solution.py:187
  164.9 306.8 %copy-start.22 = (f32[128]{0:T(128)}, f32[128]{0:T(128)S(1)}, u32[]{:S(2)}) copy-start(f32[128]{0:T(128)S(1)} %add_rsqrt_fusion) | copy-start | bytes 1540
  329.9 93.7 %copy-start.4 = (bf16[128,2048]{1,0:T(8,128)(2,1)S(1)}, bf16[128,2048]{1,0:T(8,128)(2,1)}, u32[]{:S(2)}) copy-start(bf16[128,2048]{1,0:T(8,128)(2,1)} %param.23) | copy-start | bytes 1572868
  438.0 31.5 %copy-start.2 = (bf16[128,2048]{1,0:T(8,128)(2,1)S(1)}, bf16[128,2048]{1,0:T(8,128)(2,1)}, u32[]{:S(2)}) copy-start(bf16[128,2048]{1,0:T(8,128)(2,1)} %all-reduce.5.cloned.1.call-done) | copy-start | bytes 1572868
  491.0 13.7 all-to-all-start
  496.5 43.9 %all-reduce.9.cloned.1.call-start = ((), (), s32[]{:S(2)}) async-start(), calls=%async_computation.19 | async-start | bytes 2097152 | tf_op jit(solution)/shard_map/psum | solution.py:172
  500.1 40.3 %copy-start.1 = (bf16[128,2048]{1,0:T(8,128)(2,1)S(1)}, bf16[128,2048]{1,0:T(8,128)(2,1)}, u32[]{:S(2)}) copy-start(bf16[128,2048]{1,0:T(8,128)(2,1)} %param.14) | copy-start | bytes 1572868
  500.1 40.3 %copy-start.25 = (f32[128]{0:T(128)S(1)}, f32[128]{0:T(128)}, u32[]{:S(2)}) copy-start(f32[128]{0:T(128)} %copy-done.24) | copy-start | bytes 1540
  505.1 36.8 %copy-start.21 = (f32[2048]{0:T(1024)S(1)}, f32[2048]{0:T(1024)}, u32[]{:S(2)}) copy-start(f32[2048]{0:T(1024)} %get-tuple-element.298) | copy-start | bytes 24580
  506.3 102.5 %reduce-scatter.19.cloned.1.call-start = ((), (), s32[]{:S(2)}) async-start(), calls=%async_computation.18 | async-start | bytes 1179648
  543.3 156.1 %reduce-scatter.9.cloned.1.call-start = ((), (), s32[]{:S(2)}) async-start(), calls=%async_computation.13 | async-start | bytes 4718592 | tf_op jit(solution)/shard_map/reduce_scatter | solution.py:274
  546.2 530.8 %reduce-scatter.15.cloned.1.call-start = ((), (), s32[]{:S(2)}) async-start(), calls=%async_computation.16 | async-start | bytes 25952256 | tf_op jit(solution)/shard_map/reduce_scatter | solution.py:196
  557.2 586.9 %reduce-scatter.11.cloned.1.call-start = ((), (), s32[]{:S(2)}) async-start(), calls=%async_computation.14 | async-start | bytes 1179648 | tf_op jit(solution)/shard_map/reduce_scatter | solution.py:275
  558.6 676.8 %reduce-scatter.13.cloned.1.call-start = ((), (), s32[]{:S(2)}) async-start(), calls=%async_computation.15 | async-start | bytes 4718592 | tf_op jit(solution)/shard_map/reduce_scatter | solution.py:276
  561.5 871.4 %reduce-scatter.17.cloned.1.call-start = ((), (), s32[]{:S(2)}) async-start(), calls=%async_computation.17 | async-start | bytes 12976128 | tf_op jit(solution)/shard_map/reduce_scatter | solution.py:197
  (22 other events, 62.1 us)
Sparse Core Ops, SparseCore 0:
  10.1 53.8 all-gather.5
  66.1 51.7 all-gather.7
  132.6 30.8 all-reduce.4
  166.2 163.6 all-gather.9
  331.7 91.8 all-gather.11
  438.1 31.3 all-reduce.6
  506.4 34.0 all-reduce.8
  544.8 63.9 reduce-scatter.18
  612.4 87.0 reduce-scatter.8
  703.7 373.2 reduce-scatter.14
  1081.4 62.6 reduce-scatter.10
  1148.1 87.2 reduce-scatter.12
  1240.0 192.8 reduce-scatter.16
where the time goes:
time: 1440 us
  waiting for transfers between devices  1200 us (83%)
  blocking collectives  99.3 us (7%)
  matrix products  70.4 us (5%)
  local copies, waits for them, and re-layouts  29.1 us (2%)
  other arithmetic  19.1 us (1%)
  between operations  14.4 us (1%)
    reduce_scatter x1, waiting for transfers between devices, on_device(): lax.psum_scatter(gateup_term, 'fsdp', scatter_dimension=0, tiled=True)  375 us
    reduce_scatter x1, waiting for transfers between devices, on_device(): lax.psum_scatter(down_term, 'fsdp', scatter_dimension=1, tiled=True)  197 us
    all_gather x1, waiting for transfers between devices, on_device(): lax.all_gather(w_gateup, 'fsdp', axis=0, tiled=True)  165 us
    reduce_scatter x1, waiting for transfers between devices, on_device(): lax.psum_scatter(out_term, 'fsdp', scatter_dimension=2, tiled=True)  91.4 us
    reduce_scatter x1, waiting for transfers between devices, on_device(): lax.psum_scatter(query_term, 'fsdp', scatter_dimension=0, tiled=True)  89.1 us
    all_gather x1, waiting for transfers between devices, on_device(): lax.all_gather(w_down, 'fsdp', axis=1, tiled=True)  87.5 us
    reduce_scatter x1, waiting for transfers between devices, on_device(): lax.psum_scatter(keyval_term, 'fsdp', scatter_dimension=0, tiled=True)  61.4 us
    unnamed x14, waiting for transfers between devices  39.3 us
  transfers between devices with their start and end apart: 14, of which 12 were waited for; matrix products, arithmetic and copies ran while one was open for 5% of the time, Pallas kernels for 0%

commit v1 on v0

v1 whole, which is shorter than its diff:
```python
import jax
import jax.numpy as jnp
from jax import lax
from jax.sharding import PartitionSpec as P

HD = 64
SUB = 4


epsilon = 1e-05
rope_base = 10000.0
masked_fill = -1e30
low = jnp.bfloat16
wide = jnp.float32


def locate(seq_lengths, slot_values):
    seq_ends = jnp.cumsum(seq_lengths)
    seq_starts = seq_ends - seq_lengths
    inside = (slot_values[:, None] >= seq_starts[None, :]) & (
        slot_values[:, None] < seq_ends[None, :]
    )
    first_slot = jnp.sum(jnp.where(inside, seq_starts[None, :], 0), axis=1)
    return (first_slot, slot_values - first_slot)


def rotation(position):
    half_width = HD // 2
    frequency = rope_base ** (-jnp.arange(half_width, dtype=wide) * 2.0 / HD)
    angles = position.astype(wide)[:, None] * frequency[None, :]
    return (jnp.cos(angles), jnp.sin(angles))


def rotate(values, cosine_table, sine_table):
    half_width = values.shape[-1] // 2
    table_shape = (cosine_table.shape[0],) + (1,) * (values.ndim - 2) + (half_width,)
    cosine_part = cosine_table.reshape(table_shape)
    sine_part = sine_table.reshape(table_shape)
    first_half = values[..., :half_width]
    second_half = values[..., half_width:]
    return jnp.concatenate(
        [
            first_half * cosine_part - second_half * sine_part,
            second_half * cosine_part + first_half * sine_part,
        ],
        axis=-1,
    )


def scale_of(values):
    return lax.rsqrt(jnp.mean(values * values, axis=-1, keepdims=True) + epsilon)


def norm_back(scale, normed, incoming):
    return scale * (incoming - normed * jnp.mean(incoming * normed, axis=-1, keepdims=True))


def divisor_rows(total_rows, row_limit):
    for candidate in range(min(total_rows, row_limit), 0, -1):
        if total_rows % candidate == 0:
            return candidate
    return 1


def swap(x, axis, distance):
    size = lax.axis_size(axis)
    return lax.ppermute(x, axis, [(i, i ^ distance) for i in range(size)])


def to_all(x, axis):
    size = lax.axis_size(axis)
    copies = jnp.broadcast_to(x[None], (size,) + x.shape)
    return lax.all_to_all(copies, axis, 0, 0, tiled=True)


def heads_distances():
    distances = []
    step = lax.axis_size("heads") // 2
    while step >= 1:
        distances.append(step)
        step //= 2
    return distances


def heads_gather(x):
    for distance in heads_distances():
        x = jnp.concatenate([x, swap(x, "heads", distance)], axis=0)
    return x


def heads_sum_scatter(x):
    for distance in reversed(heads_distances()):
        half = x.shape[0] // 2
        x = x[:half] + swap(x[half:].astype(low), "heads", distance).astype(wide)
    return x


def sub_gather(x):
    teams = lax.axis_size("fsdp") // SUB
    return jnp.concatenate([x] + [swap(x, "fsdp", k * teams) for k in range(1, SUB)], axis=0)


def sub_sum_scatter(x):
    teams = lax.axis_size("fsdp") // SUB
    rows = x.shape[0] // SUB
    total = x[:rows]
    for k in range(1, SUB):
        total = total + swap(
            x[k * rows : (k + 1) * rows].astype(low), "fsdp", k * teams
        ).astype(wide)
    return total


def group_gather(x):
    return heads_gather(sub_gather(x))


def group_sum_scatter(x):
    return sub_sum_scatter(heads_sum_scatter(x))


def sub_exchange(x):
    devices = lax.axis_size("fsdp")
    teams = devices // SUB
    groups = [[g * teams + t for g in range(SUB)] for t in range(teams)]
    return lax.all_to_all(x, "fsdp", 0, 0, axis_index_groups=groups, tiled=True)


def on_device(
    activations,
    norm_gains,
    w_query,
    w_keyval,
    w_out,
    w_gateup,
    w_down,
    seq_lengths,
    token_slot,
    out_grad,
):
    devices = lax.axis_size("fsdp")
    head_devices = lax.axis_size("heads")
    teams = devices // SUB
    me_heads = lax.axis_index("heads")
    me_team = lax.axis_index("fsdp") % teams
    tok_rows = activations.shape[0]
    few = tok_rows // head_devices
    width = activations.shape[1]
    cols = width // devices
    groups = w_query.shape[2] // HD
    query_width = groups * HD
    units = w_down.shape[0]
    sub_units = units // SUB

    order = [0]
    for distance in heads_distances():
        order = order + [i ^ distance for i in order]

    def reorder(x):
        blocks = x.reshape((head_devices, few) + x.shape[1:])
        return jnp.concatenate(
            [lax.dynamic_index_in_dim(blocks, me_heads ^ i, 0, keepdims=False) for i in order],
            axis=0,
        )

    qkv_shard = jnp.concatenate([w_query[:, 0], w_keyval[:, 0]], axis=1)
    qkv_w = lax.all_gather(qkv_shard, "fsdp", axis=0, tiled=True)
    out_w = lax.all_gather(w_out[0], "fsdp", axis=1, tiled=True)

    activations = reorder(activations)
    out_grad = reorder(out_grad)
    token_slot = reorder(token_slot)

    small = jnp.concatenate([norm_gains.reshape(-1).astype(wide), token_slot.astype(wide)])
    small_all = to_all(small, "fsdp")
    gains = jnp.swapaxes(small_all[:, : 2 * cols].reshape(devices, 2, cols), 0, 1).reshape(2, width)
    slot_all = small_all[:, 2 * cols :].astype(jnp.int32).reshape(-1)

    gateup_parts = jnp.stack(
        [
            jnp.swapaxes(w_gateup[:, :, k * sub_units : (k + 1) * sub_units], 0, 1)
            for k in range(SUB)
        ],
        axis=0,
    )
    gateup_here = sub_exchange(gateup_parts)
    down_here = sub_exchange(w_down.reshape(SUB, sub_units, cols))
    upstream_group = group_gather(out_grad[:few])

    def all_teams(x):
        pieces = [x] + [swap(x, "fsdp", k) for k in range(1, teams)]
        if teams == 2:
            first = me_team == 0
            return jnp.stack(
                [jnp.where(first, pieces[0], pieces[1]), jnp.where(first, pieces[1], pieces[0])],
                axis=1,
            )
        table = jnp.stack(pieces, axis=1)
        return jnp.take(table, jnp.arange(teams) ^ me_team, axis=1)

    gateup_all = all_teams(gateup_here)
    down_all = all_teams(down_here)
    gate_w = gateup_all[:, :, 0].reshape(width, sub_units)
    up_w = gateup_all[:, :, 1].reshape(width, sub_units)
    gu_w = jnp.concatenate([gate_w, up_w], axis=1)
    down_w = jnp.moveaxis(down_all, 2, 0).reshape(sub_units, width)

    first_slot, position = locate(seq_lengths, token_slot)
    cosine_table, sine_table = rotation(position)
    inputs = activations.astype(wide)
    scale_one = scale_of(inputs)
    normed_one = inputs * scale_one
    lowered_one = (normed_one * gains[0]).astype(low)
    lowered_cols = lax.all_to_all(
        jnp.swapaxes(lowered_one.reshape(tok_rows, devices, cols), 0, 1),
        "fsdp",
        0,
        0,
        tiled=True,
    ).reshape(devices * tok_rows, cols)
    qkv_lin = jnp.dot(lowered_one, qkv_w, preferred_element_type=wide)
    queries = rotate(
        qkv_lin[:, :query_width].reshape(tok_rows, groups, HD), cosine_table, sine_table
    ).astype(low)
    key_rows = rotate(
        qkv_lin[:, query_width : query_width + HD], cosine_table, sine_table
    ).astype(low)
    keyvals = jnp.concatenate([key_rows, qkv_lin[:, query_width + HD :].astype(low)], axis=-1)
    key_all = to_all(keyvals, "fsdp").reshape(devices * tok_rows, 2 * HD)
    total_keys = key_all.shape[0]
    block_rows = divisor_rows(total_keys, 1024)
    key_blocks = (
        key_all.reshape(total_keys // block_rows, block_rows, 2 * HD),
        slot_all.reshape(total_keys // block_rows, block_rows),
    )
    slot_column = token_slot[:, None]
    first_column = first_slot[:, None]

    def scores_of(key_block, slot_block):
        logits = (
            jnp.einsum("tqd,kd->tqk", queries, key_block, preferred_element_type=wide) * 0.125
        )
        allowed = (slot_block[None, :] <= slot_column) & (slot_block[None, :] >= first_column)
        return (logits, allowed[:, None, :])

    def absorb(running, blocks):
        running_max, running_sum, running_out = running
        key_block, slot_block = blocks
        logits, allowed = scores_of(key_block[:, :HD], slot_block)
        newest = jnp.maximum(running_max, jnp.max(jnp.where(allowed, logits, masked_fill), axis=-1))
        weights = jnp.where(allowed, jnp.exp(logits - newest[..., None]), 0.0)
        factor = jnp.exp(running_max - newest)
        running_sum = running_sum * factor + jnp.sum(weights, axis=-1)
        running_out = running_out * factor[..., None] + jnp.einsum(
            "tqk,kd->tqd", weights.astype(low), key_block[:, HD:], preferred_element_type=wide
        )
        return ((newest, running_sum, running_out), None)

    start_state = (
        jnp.full((tok_rows, groups), masked_fill, wide),
        jnp.zeros((tok_rows, groups), wide),
        jnp.zeros((tok_rows, groups, HD), wide),
    )
    (final_max, final_sum, final_out), unused = lax.scan(absorb, start_state, key_blocks)
    attended = final_out / final_sum[..., None]
    log_total = final_max + jnp.log(final_sum)
    attended_low = attended.reshape(tok_rows, query_width).astype(low)
    branch = heads_sum_scatter(jnp.dot(attended_low, out_w, preferred_element_type=wide))
    attended_all = to_all(attended_low, "fsdp").reshape(devices * tok_rows, query_width)

    middle = inputs[:few] + branch
    scale_two = scale_of(middle)
    normed_two = middle * scale_two
    lowered_two = (normed_two * gains[1]).astype(low)
    lowered_group = group_gather(lowered_two)
    hidden_grad = lax.dot_general(
        upstream_group, down_w, (((1,), (1,)), ((), ())), preferred_element_type=wide
    )
    gateup = jnp.dot(lowered_group, gu_w, preferred_element_type=wide)
    gate_pre = gateup[:, :sub_units]
    up_pre = gateup[:, sub_units:]
    sigmoid_gate = jax.nn.sigmoid(gate_pre)
    activated = gate_pre * sigmoid_gate
    hidden = (activated * up_pre).astype(low)
    gate_grad = hidden_grad * up_pre * sigmoid_gate * (1.0 + gate_pre * (1.0 - sigmoid_gate))
    up_grad = hidden_grad * activated
    gu_grad = jnp.concatenate([gate_grad, up_grad], axis=1).astype(low)
    lowered_grad_two = group_sum_scatter(
        lax.dot_general(gu_grad, gu_w, (((1,), (1,)), ((), ())), preferred_element_type=wide)
    )
    gain_grad_two = jnp.sum(lowered_grad_two * normed_two, axis=0)
    middle_grad = out_grad[:few].astype(wide) + norm_back(
        scale_two, normed_two, lowered_grad_two * gains[1]
    )
    branch_grad = heads_gather(middle_grad.astype(low))

    mixed = group_sum_scatter(jnp.dot(hidden, down_w, preferred_element_type=wide))
    block_out = lax.all_gather((middle + mixed).astype(low), "heads", axis=0, tiled=True)

    def teams_sum(make):
        total = make(me_team)
        for k in range(1, teams):
            total = total + swap(make(me_team ^ k).astype(low), "fsdp", k).astype(wide)
        return total

    def team_columns(x, team):
        blocks = x.reshape(x.shape[0], SUB, teams, cols)
        return lax.dynamic_index_in_dim(blocks, team, 2, keepdims=False).reshape(-1, SUB * cols)

    def gateup_term(team):
        term = lax.dot_general(
            team_columns(lowered_group, team),
            gu_grad,
            (((0,), (0,)), ((), ())),
            preferred_element_type=wide,
        )
        return term.reshape(SUB, cols, 2 * sub_units)

    def down_term(team):
        term = lax.dot_general(
            hidden,
            team_columns(upstream_group, team),
            (((0,), (0,)), ((), ())),
            preferred_element_type=wide,
        )
        return jnp.swapaxes(term.reshape(sub_units, SUB, cols), 0, 1)

    gateup_owned = sub_exchange(teams_sum(gateup_term).astype(low))
    gateup_owned = jnp.concatenate(
        [
            jnp.concatenate([gateup_owned[k, :, c * sub_units : (c + 1) * sub_units] for k in range(SUB)], axis=1)[
                :, None
            ]
            for c in range(2)
        ],
        axis=1,
    ).astype(wide)
    down_owned = sub_exchange(teams_sum(down_term).astype(low)).reshape(units, cols).astype(wide)

    branch_cols = lax.all_to_all(
        jnp.swapaxes(branch_grad.reshape(tok_rows, devices, cols), 0, 1),
        "fsdp",
        0,
        0,
        tiled=True,
    ).reshape(devices * tok_rows, cols)
    out_owned = lax.dot_general(
        attended_all, branch_cols, (((0,), (0,)), ((), ())), preferred_element_type=wide
    )[None]

    attended_grad = lax.dot_general(
        branch_grad, out_w, (((1,), (1,)), ((), ())), preferred_element_type=wide
    )
    attended_grad = attended_grad.reshape(tok_rows, groups, HD).astype(low)
    delta = jnp.sum(attended_grad.astype(wide) * attended, axis=-1)

    def backstep(query_grad, blocks):
        key_block, slot_block = blocks
        logits, allowed = scores_of(key_block[:, :HD], slot_block)
        probs = jnp.where(allowed, jnp.exp(logits - log_total[..., None]), 0.0)
        value_grad = jnp.einsum(
            "tqk,tqd->kd", probs.astype(low), attended_grad, preferred_element_type=wide
        )
        prob_grad = jnp.einsum(
            "tqd,kd->tqk", attended_grad, key_block[:, HD:], preferred_element_type=wide
        )
        score_grad = (probs * (prob_grad - delta[..., None])).astype(low)
        query_grad = query_grad + 0.125 * jnp.einsum(
            "tqk,kd->tqd", score_grad, key_block[:, :HD], preferred_element_type=wide
        )
        key_grad = 0.125 * jnp.einsum(
            "tqk,tqd->kd", score_grad, queries, preferred_element_type=wide
        )
        return (query_grad, jnp.concatenate([key_grad, value_grad], axis=-1))

    query_grad, keyval_terms = lax.scan(
        backstep, jnp.zeros((tok_rows, groups, HD), wide), key_blocks
    )
    keyval_pieces = lax.all_to_all(
        keyval_terms.reshape(devices, tok_rows, 2 * HD).astype(low), "fsdp", 0, 0, tiled=True
    )
    keyval_sum = jnp.sum(keyval_pieces.astype(wide), axis=0)
    key_unrotated = rotate(keyval_sum[:, :HD], cosine_table, -sine_table)
    keyval_grad = jnp.concatenate([key_unrotated, keyval_sum[:, HD:]], axis=-1).astype(low)
    query_lin_grad = (
        rotate(query_grad, cosine_table, -sine_table).reshape(tok_rows, query_width).astype(low)
    )
    qkv_grad = jnp.concatenate([query_lin_grad, keyval_grad], axis=1)
    lowered_part = lax.dot_general(
        qkv_grad, qkv_w, (((1,), (1,)), ((), ())), preferred_element_type=wide
    )
    gain_grad_one = jnp.sum(lowered_part * normed_one, axis=0)
    lowered_grad_one = heads_sum_scatter(lowered_part)
    input_grad = middle_grad + norm_back(
        scale_one[:few], normed_one[:few], lowered_grad_one * gains[0]
    )
    input_grad = lax.all_gather(input_grad.astype(low), "heads", axis=0, tiled=True).astype(wide)

    gain_terms = jnp.stack([gain_grad_one, gain_grad_two], axis=0)
    gain_pieces = lax.all_to_all(
        jnp.swapaxes(gain_terms.reshape(2, devices, cols), 0, 1), "fsdp", 0, 0, tiled=True
    )
    gains_owned = jnp.sum(gain_pieces, axis=0)
    for distance in heads_distances():
        gains_owned = gains_owned + swap(gains_owned, "heads", distance)

    query_all = to_all(query_lin_grad, "fsdp").reshape(devices * tok_rows, query_width)
    keyval_all = to_all(keyval_grad, "fsdp").reshape(devices * tok_rows, 2 * HD)
    query_owned = lax.dot_general(
        lowered_cols, query_all, (((0,), (0,)), ((), ())), preferred_element_type=wide
    )[:, None]
    keyval_owned = lax.dot_general(
        lowered_cols, keyval_all, (((0,), (0,)), ((), ())), preferred_element_type=wide
    )[:, None]
    return (
        block_out,
        input_grad,
        gains_owned,
        query_owned,
        keyval_owned,
        out_owned,
        gateup_owned,
        down_owned,
    )


def solution(mesh):
    placed = (
        P("fsdp", None),
        P(None, "fsdp"),
        P("fsdp", "heads", None),
        P("fsdp", "heads", None),
        P("heads", None, "fsdp"),
        P("fsdp", None, "heads"),
        P("heads", "fsdp"),
        P(),
        P("fsdp"),
        P("fsdp", None),
    )
    return jax.shard_map(
        on_device,
        mesh=mesh,
        in_specs=placed,
        out_specs=(
            P("fsdp", None),
            P("fsdp", None),
            P(None, "fsdp"),
            P("fsdp", "heads", None),
            P("fsdp", "heads", None),
            P("heads", None, "fsdp"),
            P("fsdp", None, "heads"),
            P("heads", "fsdp"),
        ),
        check_vma=False,
    )
```

time: 1440 us -> 496 us (0.34)
  waiting for transfers between devices: 1200 us -> 169 us
  starting transfers between devices: 6.44 us -> 93.9 us
  blocking collectives: 99.3 us -> 14.2 us
  local copies, waits for them, and re-layouts: 29.1 us -> 110 us
  matrix products: 70.4 us -> 43.7 us
  other arithmetic: 19.1 us -> 40.4 us
    reduce_scatter x5 -> x0, waiting for transfers between devices: 815 us -> none  [the longest x1 375 us: on_device(): lax.psum_scatter(gateup_term, 'fsdp', scatter_dimension=0, tiled=True)]
    all_gather x4 -> x2, waiting for transfers between devices: 253 us -> 46.9 us  [the longest x1 43.8 us: on_device(): out_w = lax.all_gather(w_out[0], 'fsdp', axis=1, tiled=True)]
    psum x3 -> x0, waiting for transfers between devices: 89.4 us -> none  [the longest x1 34.2 us: on_device(): lax.psum(mixed_part.astype(jnp.bfloat16), 'heads').astype(jnp.float32)]
    all_to_all x1 -> x13, waiting for transfers between devices: 4.62 us -> 90.1 us  [the longest x4 45.5 us: sub_exchange(): return lax.all_to_all(x, 'fsdp', 0, 0, axis_index_groups=groups, tiled=True)]
    all_gather x4 -> x2, blocking collectives: 99.3 us -> 14.2 us  [the longest x1 7.73 us: on_device(): lax.all_gather((middle + mixed).astype(low), 'heads', axis=0, tiled=True)]
    all_to_all x1 -> x13, starting transfers between devices: 5.52 us -> 61.8 us  [the longest x5 24.5 us: to_all(): return lax.all_to_all(copies, axis, 0, 0, tiled=True)]
    unnamed x14 -> x2, waiting for transfers between devices: 39.3 us -> 0.71 us
    ppermute x0 -> x32, starting transfers between devices: none -> 32 us  [swap(): return lax.ppermute(x, axis, [(i, i ^ distance) for i in range(size)])]
  transfers between devices with their start and end apart: 14 -> 47, of which waited for: 12 -> 21; matrix products, arithmetic and copies ran while one was open for 5% -> 34% of each run, Pallas kernels for 0% -> 0%
where the time goes in v1:
time: 496 us; the launch traced here: 488 us
  waiting for transfers between devices  169 us (34%)
  local copies, waits for them, and re-layouts  110 us (22%)
  starting transfers between devices  93.9 us (19%)
  matrix products  43.7 us (9%)
  other arithmetic  40.4 us (8%)
  between operations  15.9 us (3%)
  blocking collectives  14.2 us (3%)
    all_to_all x4, waiting for transfers between devices, sub_exchange(): return lax.all_to_all(x, 'fsdp', 0, 0, axis_index_groups=groups, tiled=True)  45.5 us
    all_gather x1, waiting for transfers between devices, on_device(): out_w = lax.all_gather(w_out[0], 'fsdp', axis=1, tiled=True)  43.8 us
    unnamed x205, local copies, waits for them, and re-layouts  41.2 us
    ppermute x32, starting transfers between devices, swap(): return lax.ppermute(x, axis, [(i, i ^ distance) for i in range(size)])  32 us
    ppermute x32, waiting for transfers between devices, swap(): return lax.ppermute(x, axis, [(i, i ^ distance) for i in range(size)])  31.6 us
    all_to_all x5, waiting for transfers between devices, to_all(): return lax.all_to_all(copies, axis, 0, 0, tiled=True)  30.5 us
    all_to_all x5, starting transfers between devices, to_all(): return lax.all_to_all(copies, axis, 0, 0, tiled=True)  24.5 us
    concatenate x17, local copies, waits for them, and re-layouts, heads_gather(): x = jnp.concatenate([x, swap(x, 'heads', distance)], axis=0)  20.5 us
  transfers between devices with their start and end apart: 47, of which 21 were waited for; matrix products, arithmetic and copies ran while one was open for 34% of the time, Pallas kernels for 0%

profile of v1, /device:TPU:0, one launch (start us, length us, event | category | flops | bytes accessed | tf_op | source)
XLA Modules:
  0.0 487.8 jit_solution(15818146909781171692)
XLA Ops:
  18.5 6.1 %all-to-all-start = ((f32[8,1,640]{2,1,0:T(1,128)}), f32[8,1,640]{2,1,0:T(1,128)S(1)}, u32[]{:S(2)}, u32[]{:S(2)}) async-start(f32[8,1,640]{2,1,0:T(1,128)} %broadcast_in_dim.125), calls=%async_computation | async-start | bytes 40960 | tf_op jit(solution)/shard_map/all_to_all | solution.py:73
  38.1 5.5 %all-to-all-start.3 = ((bf16[4,352,256]{2,1,0:T(8,128)(2,1)}), bf16[4,352,256]{2,1,0:T(8,128)(2,1)S(1)}, u32[]{:S(2)}, u32[]{:S(2)}) async-start(bf16[4,352,256]{2,1,0:T(8,128)(2,1)} %bitcast.268), calls=%async_computation.3 | async-start | bytes 1441792 | tf_op jit(solution)/shard_map/all_to_all | solution.py:126
  51.3 5.1 %collective-permute-done.17 = bf16[128,2048]{1,0:T(8,128)(2,1)S(1)} collective-permute-done((bf16[128,2048]{1,0:T(8,128)(2,1)S(1)}, bf16[128,2048]{1,0:T(8,128)(2,1)S(1)}, u32[]{:S(2)}, u32[]{:S(2)}) %collective-permute-start.17) | collective-permute-done | bytes 524320 | tf_op jit(solution)/shard_map/ppermute | solution.py:67
  58.6 19.0 %all-to-all-done.3 = bf16[4,352,256]{2,1,0:T(8,128)(2,1)S(1)} async-done(((bf16[4,352,256]{2,1,0:T(8,128)(2,1)}), bf16[4,352,256]{2,1,0:T(8,128)(2,1)S(1)}, u32[]{:S(2)}, u32[]{:S(2)}) %all-to-all-start.3) | async-done | bytes 720928 | tf_op jit(solution)/shard_map/all_to_all | solution.py:126
  93.0 8.9 %all-to-all-done.1 = bf16[8,128,128]{1,2,0:T(8,128)(2,1)S(1)} async-done(((bf16[8,128,128]{1,2,0:T(8,128)(2,1)}), bf16[8,128,128]{1,2,0:T(8,128)(2,1)S(1)}, u32[]{:S(2)}, u32[]{:S(2)}) %all-to-all-start.1) | async-done | bytes 262176 | tf_op jit(solution)/shard_map/all_to_all | solution.py:73
  101.9 5.0 %all-to-all-start.2 = ((bf16[4,2,256,352]{2,3,1,0:T(8,128)(2,1)}), bf16[4,2,256,352]{2,3,1,0:T(8,128)(2,1)}, u32[]{:S(2)}, u32[]{:S(2)}) async-start(bf16[4,2,256,352]{2,3,1,0:T(8,128)(2,1)} %pad_maximum_fusion.1), calls=%async_computation.2 | async-start | bytes 2883584 | tf_op jit(solution)/shard_map/all_to_all | solution.py:126
  111.8 43.8 %all-gather.6.cloned.1.call-done = bf16[1,512,2048]{2,1,0:T(8,128)(2,1)} async-done(((bf16[1,512,256]{2,1,0:T(8,128)(2,1)}), bf16[1,512,2048]{2,1,0:T(8,128)(2,1)}) %all-gather.6.cloned.1.call-update) | async-done | bytes 2097168 | tf_op jit(solution)/shard_map/all_gather | solution.py:168
  174.7 7.3 %collective-permute-done.3 = bf16[32,2048]{1,0:T(8,128)(2,1)S(1)} collective-permute-done((bf16[32,2048]{1,0:T(8,128)(2,1)S(1)}, bf16[32,2048]{1,0:T(8,128)(2,1)S(1)}, u32[]{:S(2)}, u32[]{:S(2)}) %collective-permute-start.3) | collective-permute-done | bytes 131104 | tf_op jit(solution)/shard_map/ppermute | solution.py:67
  184.7 8.6 %collective-permute-done.5 = bf16[128,2048]{1,0:T(8,128)(2,1)S(1)} collective-permute-done((bf16[128,2048]{1,0:T(8,128)(2,1)S(1)}, bf16[128,2048]{1,0:T(8,128)(2,1)S(1)}, u32[]{:S(2)}, u32[]{:S(2)}) %collective-permute-start.5) | collective-permute-done | bytes 524320 | tf_op jit(solution)/shard_map/ppermute | solution.py:67
  211.2 4.6 reshape_squeeze.7
  235.9 6.1 %all-to-all-start.6 = ((bf16[8,128,256]{1,2,0:T(8,128)(2,1)}), bf16[8,128,256]{1,2,0:T(8,128)(2,1)S(1)}, u32[]{:S(2)}, u32[]{:S(2)}) async-start(bf16[8,128,256]{1,2,0:T(8,128)(2,1)} %fusion.47), calls=%async_computation.6 | async-start | bytes 1048576 | tf_op jit(solution)/shard_map/all_to_all | solution.py:214
  251.6 5.5 %concatenate.153 = bf16[512,4,2,256]{0,3,1,2:T(8,128)(2,1)} concatenate(bf16[32,4,2,256]{0,3,1,2:T(8,128)(2,1)} %copy.201, bf16[32,4,2,256]{0,3,1,2:T(8,128)(2,1)} %copy.202, bf16[32,4,2,256]{0,3,1,2:T(8,128)(2,1)} %copy.203, bf16[32,4,2,256]{0,3,1,2:T(8,128)(2,1)} %copy.204, bf16[128,4,2,256]{0,3,1,2:T(8,128)(2,1)} %copy.205, bf16[256,4,2,256]{0,3,1,2:T(8,128)(2,1)S(1)} %copy.206), dimensions={0} | concatenate | bytes 4194304 | tf_op jit(solution)/shard_map/concatenate | solution.py:87
  272.5 6.3 %constant_dynamic-slice_fusion.1 = (bf16[512,4,1,256]{3,2,1,0:T(2,128)(2,1)}, bf16[512,4,1,256]{3,2,1,0:T(2,128)(2,1)}) fusion(bf16[512,4,2,256]{3,2,1,0:T(2,128)(2,1)S(1)} %reshape.427, s32[]{:T(128)S(6)} %select_n.91, s32[]{:T(128)S(6)} %select_n.92), kind=kLoop, calls=%fused_computation.201 | loop fusion | bytes 4194312 | tf_op jit(solution)/shard_map/jit(dynamic_index_in_dim)/dynamic_slice | solution.py:308
  278.9 4.6 copy.219
  293.2 5.8 %all-to-all-start.9 = ((bf16[8,128,512]{1,2,0:T(8,128)(2,1)}), bf16[8,128,512]{1,2,0:T(8,128)(2,1)}, u32[]{:S(2)}, u32[]{:S(2)}) async-start(bf16[8,128,512]{1,2,0:T(8,128)(2,1)} %broadcast_in_dim.135), calls=%async_computation.9 | async-start | bytes 2097152 | tf_op jit(solution)/shard_map/all_to_all | solution.py:73
  313.6 20.2 %all-to-all-done.9 = bf16[8,128,512]{1,2,0:T(8,128)(2,1)} async-done(((bf16[8,128,512]{1,2,0:T(8,128)(2,1)}), bf16[8,128,512]{1,2,0:T(8,128)(2,1)}, u32[]{:S(2)}, u32[]{:S(2)}) %all-to-all-start.9) | async-done | bytes 1048608 | tf_op jit(solution)/shard_map/all_to_all | solution.py:73
  357.2 7.6 %all-to-all-done.12 = bf16[4,352,256]{2,1,0:T(8,128)(2,1)S(1)} async-done(((bf16[4,352,256]{2,1,0:T(8,128)(2,1)}), bf16[4,352,256]{2,1,0:T(8,128)(2,1)S(1)}, u32[]{:S(2)}, u32[]{:S(2)}) %all-to-all-start.12) | async-done | bytes 720928 | tf_op jit(solution)/shard_map/all_to_all | solution.py:126
  370.0 4.7 all-to-all-done.5
  384.0 5.6 %all-to-all-done.10 = bf16[8,128,256]{2,1,0:T(8,128)(2,1)} async-done(((bf16[8,128,256]{2,1,0:T(8,128)(2,1)}), bf16[8,128,256]{2,1,0:T(8,128)(2,1)}, u32[]{:S(2)}, u32[]{:S(2)}) %all-to-all-start.10) | async-done | bytes 524320 | tf_op jit(solution)/shard_map/all_to_all | solution.py:340
  402.2 5.2 %all-to-all-start.11 = ((bf16[4,256,704]{1,2,0:T(8,128)(2,1)}), bf16[4,256,704]{1,2,0:T(8,128)(2,1)}, u32[]{:S(2)}, u32[]{:S(2)}) async-start(bf16[4,256,704]{1,2,0:T(8,128)(2,1)} %add_convert_fusion), calls=%async_computation.11 | async-start | bytes 2883584 | tf_op jit(solution)/shard_map/all_to_all | solution.py:126
  426.0 18.9 %all-to-all-done.11 = bf16[4,256,704]{1,2,0:T(8,128)(2,1)} async-done(((bf16[4,256,704]{1,2,0:T(8,128)(2,1)}), bf16[4,256,704]{1,2,0:T(8,128)(2,1)}, u32[]{:S(2)}, u32[]{:S(2)}) %all-to-all-start.11) | async-done | bytes 1441824 | tf_op jit(solution)/shard_map/all_to_all | solution.py:126
  446.0 5.3 %all-to-all-start.7 = ((bf16[8,128,512]{2,1,0:T(8,128)(2,1)}), bf16[8,128,512]{2,1,0:T(8,128)(2,1)}, u32[]{:S(2)}, u32[]{:S(2)}) async-start(bf16[8,128,512]{2,1,0:T(8,128)(2,1)} %broadcast_in_dim.131), calls=%async_computation.7 | async-start | bytes 2097152 | tf_op jit(solution)/shard_map/all_to_all | solution.py:73
  452.6 6.5 %all_gather.15 = bf16[128,2048]{1,0:T(8,128)(2,1)S(1)} all-gather(bf16[32,2048]{1,0:T(8,128)(2,1)S(1)} %get-tuple-element.176), channel_id=1, replica_groups=mesh['fsdp'=8,'heads'=4] {'heads'}, dimensions={0}, use_global_device_ids=true | all-gather | bytes 655360 | tf_op jit(solution)/shard_map/all_gather | solution.py:397
  460.2 7.7 %all_gather.14 = bf16[128,2048]{1,0:T(8,128)(2,1)} all-gather(bf16[32,2048]{1,0:T(8,128)(2,1)S(1)} %get-tuple-element.177), channel_id=1, replica_groups=mesh['fsdp'=8,'heads'=4] {'heads'}, dimensions={0}, use_global_device_ids=true | all-gather | bytes 655360 | tf_op jit(solution)/shard_map/all_gather | solution.py:298
  (426 shorter events, 248.2 us)
Async XLA Ops:
  7.2 73.7 %all-gather.4.cloned.1.call-start = ((), (), s32[]{:S(2)}) async-start(), calls=%async_computation.13 | async-start | bytes 2949120 | tf_op jit(solution)/shard_map/all_gather | solution.py:167
  10.8 33.5 %collective-permute-start.14 = (bf16[32,2048]{1,0:T(8,128)(2,1)S(1)}, bf16[32,2048]{1,0:T(8,128)(2,1)S(1)}, u32[]{:S(2)}, u32[]{:S(2)}) collective-permute-start(bf16[32,2048]{1,0:T(8,128)(2,1)S(1)} %bitcast.236), channel_id=1, source_target_pairs={{0,8},{4,12},{8,0},{12,4},{16,24},{20,28},{24,16},{28,20},{1,9},{5... | collective-permute-start | bytes 393224 | tf_op jit(solution)/shard_map/ppermute | solution.py:67
  13.8 30.5 %collective-permute-start.15 = (bf16[32,2048]{1,0:T(8,128)(2,1)S(1)}, bf16[32,2048]{1,0:T(8,128)(2,1)S(1)}, u32[]{:S(2)}, u32[]{:S(2)}) collective-permute-start(bf16[32,2048]{1,0:T(8,128)(2,1)S(1)} %bitcast.237), channel_id=1, source_target_pairs={{0,16},{4,20},{8,24},{12,28},{16,0},{20,4},{24,8},{28,12},{1,17},{... | collective-permute-start | bytes 393224 | tf_op jit(solution)/shard_map/ppermute | solution.py:67
  16.4 27.9 %collective-permute-start.16 = (bf16[32,2048]{1,0:T(8,128)(2,1)S(1)}, bf16[32,2048]{1,0:T(8,128)(2,1)}, u32[]{:S(2)}, u32[]{:S(2)}) collective-permute-start(bf16[32,2048]{1,0:T(8,128)(2,1)S(1)} %bitcast.238), channel_id=1, source_target_pairs={{0,24},{4,28},{8,16},{12,20},{16,8},{20,12},{24,0},{28,4},{1,25},{... | collective-permute-start | bytes 393224 | tf_op jit(solution)/shard_map/ppermute | solution.py:67
  18.5 19.6 %all-to-all-start = ((f32[8,1,640]{2,1,0:T(1,128)}), f32[8,1,640]{2,1,0:T(1,128)S(1)}, u32[]{:S(2)}, u32[]{:S(2)}) async-start(f32[8,1,640]{2,1,0:T(1,128)} %broadcast_in_dim.125), calls=%async_computation | async-start | bytes 40960 | tf_op jit(solution)/shard_map/all_to_all | solution.py:73
  24.6 131.0 %all-gather.6.cloned.1.call-start = ((), (), s32[]{:S(2)}) async-start(), calls=%async_computation.14 | async-start | bytes 2359296 | tf_op jit(solution)/shard_map/all_gather | solution.py:168
  38.1 39.4 %all-to-all-start.3 = ((bf16[4,352,256]{2,1,0:T(8,128)(2,1)}), bf16[4,352,256]{2,1,0:T(8,128)(2,1)S(1)}, u32[]{:S(2)}, u32[]{:S(2)}) async-start(bf16[4,352,256]{2,1,0:T(8,128)(2,1)} %bitcast.268), calls=%async_computation.3 | async-start | bytes 1441792 | tf_op jit(solution)/shard_map/all_to_all | solution.py:126
  58.4 31.5 %collective-permute-start.18 = (bf16[256,2048]{1,0:T(8,128)(2,1)}, bf16[256,2048]{1,0:T(8,128)(2,1)S(1)}, u32[]{:S(2)}, u32[]{:S(2)}) collective-permute-start(bf16[256,2048]{1,0:T(8,128)(2,1)} %copy-done.69), channel_id=1, source_target_pairs={{0,1},{1,0},{2,3},{3,2},{4,5},{5,4},{6,7},{7,6},{8,9},{9,8},{10,11... | collective-permute-start | bytes 3145736 | tf_op jit(solution)/shard_map/ppermute | solution.py:67
  77.6 80.2 %collective-permute-start.8 = (bf16[4,352,256]{2,1,0:T(8,128)(2,1)S(1)}, bf16[4,352,256]{2,1,0:T(8,128)(2,1)}, u32[]{:S(2)}, u32[]{:S(2)}) collective-permute-start(bf16[4,352,256]{2,1,0:T(8,128)(2,1)S(1)} %all-to-all-done.3), channel_id=1, source_target_pairs={{0,4},{4,0},{8,12},{12,8},{16,20},{20,16},{24,28},{28,24},{1,5},{5... | collective-permute-start | bytes 2162696 | tf_op jit(solution)/shard_map/ppermute | solution.py:67
  101.9 62.4 %all-to-all-start.2 = ((bf16[4,2,256,352]{2,3,1,0:T(8,128)(2,1)}), bf16[4,2,256,352]{2,3,1,0:T(8,128)(2,1)}, u32[]{:S(2)}, u32[]{:S(2)}) async-start(bf16[4,2,256,352]{2,3,1,0:T(8,128)(2,1)} %pad_maximum_fusion.1), calls=%async_computation.2 | async-start | bytes 2883584 | tf_op jit(solution)/shard_map/all_to_all | solution.py:126
  164.3 33.6 %collective-permute-start.7 = (bf16[4,2,256,352]{2,3,1,0:T(8,128)(2,1)}, bf16[4,2,256,352]{2,3,1,0:T(8,128)(2,1)S(1)}, u32[]{:S(2)}, u32[]{:S(2)}) collective-permute-start(bf16[4,2,256,352]{2,3,1,0:T(8,128)(2,1)} %all-to-all-done.2), channel_id=1, source_target_pairs={{0,4},{4,0},{8,12},{12,8},{16,20},{20,16},{24,28},{28,24},{1,5},{5... | collective-permute-start | bytes 4325384 | tf_op jit(solution)/shard_map/ppermute | solution.py:67
  194.2 23.1 %collective-permute-start.6 = (bf16[256,2048]{1,0:T(8,128)(2,1)}, bf16[256,2048]{1,0:T(8,128)(2,1)}, u32[]{:S(2)}, u32[]{:S(2)}) collective-permute-start(bf16[256,2048]{1,0:T(8,128)(2,1)} %get-tuple-element.164), channel_id=1, source_target_pairs={{0,1},{1,0},{2,3},{3,2},{4,5},{5,4},{6,7},{7,6},{8,9},{9,8},{10,11... | collective-permute-start | bytes 3145736 | tf_op jit(solution)/shard_map/ppermute | solution.py:67
  231.3 33.9 %collective-permute-start.20 = (bf16[128,2048]{1,0:T(8,128)(2,1)}, bf16[128,2048]{1,0:T(8,128)(2,1)}, u32[]{:S(2)}, u32[]{:S(2)}) collective-permute-start(bf16[128,2048]{1,0:T(8,128)(2,1)} %slice.420), channel_id=1, source_target_pairs={{0,2},{1,3},{2,0},{3,1},{4,6},{5,7},{6,4},{7,5},{8,10},{9,11},{10,... | collective-permute-start | bytes 1572872 | tf_op jit(solution)/shard_map/ppermute | solution.py:67
  235.9 56.1 %all-to-all-start.6 = ((bf16[8,128,256]{1,2,0:T(8,128)(2,1)}), bf16[8,128,256]{1,2,0:T(8,128)(2,1)S(1)}, u32[]{:S(2)}, u32[]{:S(2)}) async-start(bf16[8,128,256]{1,2,0:T(8,128)(2,1)} %fusion.47), calls=%async_computation.6 | async-start | bytes 1048576 | tf_op jit(solution)/shard_map/all_to_all | solution.py:214
  263.2 75.1 %collective-permute-start.31 = (bf16[4,352,256]{2,1,0:T(8,128)(2,1)}, bf16[4,352,256]{2,1,0:T(8,128)(2,1)}, u32[]{:S(2)}, u32[]{:S(2)}) collective-permute-start(bf16[4,352,256]{2,1,0:T(8,128)(2,1)} %fusion.14), channel_id=1, source_target_pairs={{0,4},{4,0},{8,12},{12,8},{16,20},{20,16},{24,28},{28,24},{1,5},{5... | collective-permute-start | bytes 2162696 | tf_op jit(solution)/shard_map/ppermute | solution.py:67
  290.8 107.4 %collective-permute-start.30 = (bf16[4,256,704]{1,2,0:T(8,128)(2,1)}, bf16[4,256,704]{1,2,0:T(8,128)(2,1)}, u32[]{:S(2)}, u32[]{:S(2)}) collective-permute-start(bf16[4,256,704]{1,2,0:T(8,128)(2,1)} %convolution_convert_fusion), channel_id=1, source_target_pairs={{0,4},{4,0},{8,12},{12,8},{16,20},{20,16},{24,28},{28,24},{1,5},{5... | collective-permute-start | bytes 4325384 | tf_op jit(solution)/shard_map/ppermute | solution.py:67
  293.2 40.6 %all-to-all-start.9 = ((bf16[8,128,512]{1,2,0:T(8,128)(2,1)}), bf16[8,128,512]{1,2,0:T(8,128)(2,1)}, u32[]{:S(2)}, u32[]{:S(2)}) async-start(bf16[8,128,512]{1,2,0:T(8,128)(2,1)} %broadcast_in_dim.135), calls=%async_computation.9 | async-start | bytes 2097152 | tf_op jit(solution)/shard_map/all_to_all | solution.py:73
  303.5 75.4 %collective-permute-start.9 = (bf16[256,2048]{1,0:T(8,128)(2,1)}, bf16[256,2048]{1,0:T(8,128)(2,1)}, u32[]{:S(2)}, u32[]{:S(2)}) collective-permute-start(bf16[256,2048]{1,0:T(8,128)(2,1)} %slice.419), channel_id=1, source_target_pairs={{0,1},{1,0},{2,3},{3,2},{4,5},{5,4},{6,7},{7,6},{8,9},{9,8},{10,11... | collective-permute-start | bytes 3145736 | tf_op jit(solution)/shard_map/ppermute | solution.py:67
  383.3 24.1 %collective-permute-start.10 = (bf16[128,2048]{1,0:T(8,128)(2,1)}, bf16[128,2048]{1,0:T(8,128)(2,1)}, u32[]{:S(2)}, u32[]{:S(2)}) collective-permute-start(bf16[128,2048]{1,0:T(8,128)(2,1)} %slice.421), channel_id=1, source_target_pairs={{0,2},{1,3},{2,0},{3,1},{4,6},{5,7},{6,4},{7,5},{8,10},{9,11},{10,... | collective-permute-start | bytes 1572872 | tf_op jit(solution)/shard_map/ppermute | solution.py:67
  402.2 42.7 %all-to-all-start.11 = ((bf16[4,256,704]{1,2,0:T(8,128)(2,1)}), bf16[4,256,704]{1,2,0:T(8,128)(2,1)}, u32[]{:S(2)}, u32[]{:S(2)}) async-start(bf16[4,256,704]{1,2,0:T(8,128)(2,1)} %add_convert_fusion), calls=%async_computation.11 | async-start | bytes 2883584 | tf_op jit(solution)/shard_map/all_to_all | solution.py:126
  413.4 37.9 %collective-permute-start.11 = (bf16[32,2048]{1,0:T(8,128)(2,1)}, bf16[32,2048]{1,0:T(8,128)(2,1)S(1)}, u32[]{:S(2)}, u32[]{:S(2)}) collective-permute-start(bf16[32,2048]{1,0:T(8,128)(2,1)} %get-tuple-element.161), channel_id=1, source_target_pairs={{0,8},{4,12},{8,0},{12,4},{16,24},{20,28},{24,16},{28,20},{1,9},{5... | collective-permute-start | bytes 393224 | tf_op jit(solution)/shard_map/ppermute | solution.py:67
  415.4 35.9 %collective-permute-start.12 = (bf16[32,2048]{1,0:T(8,128)(2,1)S(1)}, bf16[32,2048]{1,0:T(8,128)(2,1)S(1)}, u32[]{:S(2)}, u32[]{:S(2)}) collective-permute-start(bf16[32,2048]{1,0:T(8,128)(2,1)S(1)} %get-tuple-element.163), channel_id=1, source_target_pairs={{0,16},{4,20},{8,24},{12,28},{16,0},{20,4},{24,8},{28,12},{1,17},{... | collective-permute-start | bytes 393224 | tf_op jit(solution)/shard_map/ppermute | solution.py:67
  417.7 33.5 %collective-permute-start.13 = (bf16[32,2048]{1,0:T(8,128)(2,1)S(1)}, bf16[32,2048]{1,0:T(8,128)(2,1)S(1)}, u32[]{:S(2)}, u32[]{:S(2)}) collective-permute-start(bf16[32,2048]{1,0:T(8,128)(2,1)S(1)} %get-tuple-element.162), channel_id=1, source_target_pairs={{0,24},{4,28},{8,16},{12,20},{16,8},{20,12},{24,0},{28,4},{1,25},{... | collective-permute-start | bytes 393224 | tf_op jit(solution)/shard_map/ppermute | solution.py:67
  446.0 30.7 %all-to-all-start.7 = ((bf16[8,128,512]{2,1,0:T(8,128)(2,1)}), bf16[8,128,512]{2,1,0:T(8,128)(2,1)}, u32[]{:S(2)}, u32[]{:S(2)}) async-start(bf16[8,128,512]{2,1,0:T(8,128)(2,1)} %broadcast_in_dim.131), calls=%async_computation.7 | async-start | bytes 2097152 | tf_op jit(solution)/shard_map/all_to_all | solution.py:73
  (114 other events, 1778.5 us)
Sparse Core Ops, SparseCore 0:
  10.8 70.0 all-gather.3
  83.0 72.6 all-gather.5

commit v2 on v1

v2 whole, which is shorter than its diff:
```python
import jax
import jax.numpy as jnp
from jax import lax
from jax.sharding import PartitionSpec as P

HD = 64
SUB = 4


epsilon = 1e-05
rope_base = 10000.0
masked_fill = -1e30
low = jnp.bfloat16
wide = jnp.float32


def locate(seq_lengths, slot_values):
    seq_ends = jnp.cumsum(seq_lengths)
    seq_starts = seq_ends - seq_lengths
    inside = (slot_values[:, None] >= seq_starts[None, :]) & (
        slot_values[:, None] < seq_ends[None, :]
    )
    first_slot = jnp.sum(jnp.where(inside, seq_starts[None, :], 0), axis=1)
    return (first_slot, slot_values - first_slot)


def rotation(position):
    half_width = HD // 2
    frequency = rope_base ** (-jnp.arange(half_width, dtype=wide) * 2.0 / HD)
    angles = position.astype(wide)[:, None] * frequency[None, :]
    return (jnp.cos(angles), jnp.sin(angles))


def rotate(values, cosine_table, sine_table):
    half_width = values.shape[-1] // 2
    table_shape = (cosine_table.shape[0],) + (1,) * (values.ndim - 2) + (half_width,)
    cosine_part = cosine_table.reshape(table_shape)
    sine_part = sine_table.reshape(table_shape)
    first_half = values[..., :half_width]
    second_half = values[..., half_width:]
    return jnp.concatenate(
        [
            first_half * cosine_part - second_half * sine_part,
            second_half * cosine_part + first_half * sine_part,
        ],
        axis=-1,
    )


def scale_of(values):
    return lax.rsqrt(jnp.mean(values * values, axis=-1, keepdims=True) + epsilon)


def norm_back(scale, normed, incoming):
    return scale * (incoming - normed * jnp.mean(incoming * normed, axis=-1, keepdims=True))


def divisor_rows(total_rows, row_limit):
    for candidate in range(min(total_rows, row_limit), 0, -1):
        if total_rows % candidate == 0:
            return candidate
    return 1


def swap(x, axis, distance):
    size = lax.axis_size(axis)
    return lax.ppermute(x, axis, [(i, i ^ distance) for i in range(size)])


def after(x, *others):
    return lax.optimization_barrier((x,) + others)[0]


def to_all(x, axis):
    size = lax.axis_size(axis)
    copies = jnp.broadcast_to(x[None], (size,) + x.shape)
    return lax.all_to_all(copies, axis, 0, 0, tiled=True)


def heads_distances():
    distances = []
    step = lax.axis_size("heads") // 2
    while step >= 1:
        distances.append(step)
        step //= 2
    return distances


def sub_distances():
    teams = lax.axis_size("fsdp") // SUB
    return [k * teams for k in range(1, SUB)]


def sub_gather(x):
    return jnp.concatenate([x] + [swap(x, "fsdp", d) for d in sub_distances()], axis=0)


def heads_gather(x, earlier=()):
    *others, last = heads_distances()
    for distance in others:
        x = jnp.concatenate([x, swap(x, "heads", distance)], axis=0)
    if earlier:
        x = after(x, *earlier)
    return jnp.concatenate([x, swap(x, "heads", last)], axis=0)


def group_gather(x, earlier=()):
    x = sub_gather(x)
    if earlier:
        x = after(x, *earlier)
    return heads_gather(x)


def group_blocks():
    blocks = [(k, 0) for k in range(SUB)]
    for distance in heads_distances():
        blocks = blocks + [(k, d ^ distance) for k, d in blocks]
    return blocks


def first_sum(make, rows):
    half = rows // 2
    distance = heads_distances()[-1]
    away = swap(make(half, rows).astype(low), "heads", distance)
    return make(0, half) + away.astype(wide)


def other_sums(x):
    for distance in reversed(heads_distances()[:-1]):
        half = x.shape[0] // 2
        x = x[:half] + swap(x[half:].astype(low), "heads", distance).astype(wide)
    return x


def sub_sum(x):
    few = x.shape[0] // SUB
    total = x[:few]
    for k, distance in enumerate(sub_distances()):
        away = swap(x[(k + 1) * few : (k + 2) * few].astype(low), "fsdp", distance)
        total = total + away.astype(wide)
    return total


def sub_exchange(x):
    devices = lax.axis_size("fsdp")
    teams = devices // SUB
    groups = [[g * teams + t for g in range(SUB)] for t in range(teams)]
    return lax.all_to_all(x, "fsdp", 0, 0, axis_index_groups=groups, tiled=True)


def teams_pieces(x):
    teams = lax.axis_size("fsdp") // SUB
    return [x] + [swap(x, "fsdp", k) for k in range(1, teams)]


def own_team_first(x):
    teams = lax.axis_size("fsdp") // SUB
    me_team = lax.axis_index("fsdp") % teams
    blocks = x.reshape(x.shape[0], SUB, teams, -1)
    if teams == 2:
        first, second = (blocks[:, :, t].reshape(x.shape[0], -1) for t in range(2))
        swapped = me_team == 1
        return jnp.concatenate(
            [jnp.where(swapped, second, first), jnp.where(swapped, first, second)], axis=1
        )
    blocks = jnp.take(blocks, jnp.arange(teams) ^ me_team, axis=2)
    return jnp.swapaxes(blocks, 1, 2).reshape(x.shape)


def teams_in_place(x):
    teams = lax.axis_size("fsdp") // SUB
    me_team = lax.axis_index("fsdp") % teams
    blocks = x.reshape(x.shape[0], teams, SUB, -1)
    if teams == 2:
        swapped = me_team == 1
        pair = [
            jnp.where(swapped, blocks[:, 1], blocks[:, 0]),
            jnp.where(swapped, blocks[:, 0], blocks[:, 1]),
        ]
        return jnp.stack(pair, axis=2).reshape(x.shape)
    blocks = jnp.take(blocks, jnp.arange(teams) ^ me_team, axis=1)
    return jnp.swapaxes(blocks, 1, 2).reshape(x.shape)


def teams_sum(make):
    teams = lax.axis_size("fsdp") // SUB
    away = [swap(make(k).astype(low), "fsdp", k) for k in range(1, teams)]
    total = make(0)
    for piece in away:
        total = total + piece.astype(wide)
    return total.astype(low)


def wider(x, size, axis):
    missing = [(0, 0)] * x.ndim
    missing[axis] = (0, size - x.shape[axis])
    return jnp.pad(x, missing)


def over_rows(left, right):
    return lax.dot_general(left, right, (((0,), (0,)), ((), ())), preferred_element_type=wide)


def over_cols(left, right):
    return lax.dot_general(left, right, (((1,), (1,)), ((), ())), preferred_element_type=wide)


def on_device(
    activations,
    norm_gains,
    w_query,
    w_keyval,
    w_out,
    w_gateup,
    w_down,
    seq_lengths,
    token_slot,
    out_grad,
):
    devices = lax.axis_size("fsdp")
    head_devices = lax.axis_size("heads")
    teams = devices // SUB
    me_heads = lax.axis_index("heads")
    me_team = lax.axis_index("fsdp") % teams
    me_sub = lax.axis_index("fsdp") // teams
    tok_rows, width = activations.shape
    few = tok_rows // head_devices
    rows = SUB * tok_rows
    cols = width // devices
    groups = w_query.shape[2] // HD // SUB
    query_width = groups * HD
    units = w_down.shape[0]
    sub_units = -(-units // (SUB * 128)) * 128
    qkv_width = query_width + 2 * HD
    lanes = max(qkv_width, cols)
    team_width = SUB * cols

    def share(x):
        return lax.dynamic_slice_in_dim(x, me_heads * few, few, 0)

    x_sub = sub_gather(own_team_first(share(activations)))

    extras = jnp.concatenate(
        [
            wider(norm_gains, lanes, 1),
            wider((token_slot // 128).astype(low)[None], lanes, 1),
            wider((token_slot % 128).astype(low)[None], lanes, 1),
            jnp.zeros((12, lanes), low),
        ],
        axis=0,
    )
    extras = lax.optimization_barrier(extras)
    attention_parts = jnp.stack(
        [
            jnp.concatenate(
                [
                    wider(
                        jnp.concatenate(
                            [
                                w_query[:, 0, k * query_width : (k + 1) * query_width],
                                w_keyval[:, 0],
                            ],
                            axis=1,
                        ),
                        lanes,
                        1,
                    ),
                    extras,
                ],
                axis=0,
            )
            for k in range(SUB)
        ],
        axis=0,
    )
    attention_here = sub_exchange(attention_parts)
    attention_pieces = teams_pieces(attention_here)
    x_group = heads_gather(x_sub, (attention_here,))
    qkv_w = jnp.concatenate(
        [piece[:, :cols, :qkv_width].reshape(team_width, qkv_width) for piece in attention_pieces],
        axis=0,
    )
    extras_all = jnp.stack([piece[:, cols:] for piece in attention_pieces], axis=0)
    gains = jnp.swapaxes(extras_all[:, :, :2, :cols].reshape(devices, 2, cols), 0, 1)
    gains = gains.reshape(2, width).astype(wide)
    slot_parts = extras_all[:, :, 2:4, :tok_rows].astype(jnp.int32)
    slot_blocks = (slot_parts[:, :, 0] * 128 + slot_parts[:, :, 1]).reshape(
        devices * head_devices, few
    )
    block_places = [
        ((t * SUB + (me_sub ^ k)) * head_devices) + (me_heads ^ d)
        for t in range(teams)
        for k, d in group_blocks()
    ]
    slot_all = jnp.take(slot_blocks, jnp.stack(block_places), axis=0).reshape(teams * rows)
    slot_group = slot_all[:rows]

    tall_parts = jnp.concatenate(
        [
            w_out[0].reshape(SUB, query_width, cols),
            wider(w_down, SUB * sub_units, 0).reshape(SUB, sub_units, cols),
        ],
        axis=1,
    )
    tall_here = sub_exchange(after(tall_parts, attention_here))
    tall_pieces = teams_pieces(tall_here)
    out_w = jnp.concatenate(
        [piece[z, :query_width] for piece in tall_pieces for z in range(SUB)], axis=1
    )
    down_w = jnp.concatenate(
        [piece[z, query_width:] for piece in tall_pieces for z in range(SUB)], axis=1
    )
    gateup_parts = wider(w_gateup, SUB * sub_units, 2)
    gateup_parts = jnp.stack(
        [
            jnp.concatenate(
                [gateup_parts[:, c, k * sub_units : (k + 1) * sub_units] for c in range(2)], axis=1
            )
            for k in range(SUB)
        ],
        axis=0,
    )
    gateup_here = sub_exchange(after(gateup_parts, tall_here))
    half_sub = SUB // 2
    gateup_halves = [
        [swap(part, "fsdp", k) for k in range(1, teams)]
        for part in (gateup_here[:half_sub], gateup_here[half_sub:])
    ]
    gateup_pieces = [gateup_here] + [jnp.concatenate(pair, axis=0) for pair in zip(*gateup_halves)]
    upstream_share = own_team_first(share(out_grad))
    upstream_sub = sub_gather(after(upstream_share, x_sub))
    upstream_group = heads_gather(upstream_sub)

    first_slot, position = locate(seq_lengths, slot_group)
    cosine_table, sine_table = rotation(position)
    inputs = x_group.astype(wide)
    scale_one = scale_of(inputs)
    normed_one = inputs * scale_one
    lowered_one = after((normed_one * gains[0]).astype(low), x_group)
    qkv_lin = jnp.dot(lowered_one, qkv_w, preferred_element_type=wide)
    queries = rotate(
        qkv_lin[:, :query_width].reshape(rows, groups, HD), cosine_table, sine_table
    ).astype(low)
    queries = after(queries, tall_here, upstream_sub)
    key_rows = rotate(
        qkv_lin[:, query_width : query_width + HD], cosine_table, sine_table
    ).astype(low)
    keyvals = jnp.concatenate([key_rows, qkv_lin[:, query_width + HD :].astype(low)], axis=-1)
    key_all = jnp.concatenate(
        [keyvals] + [swap(keyvals, "fsdp", k) for k in range(1, teams)], axis=0
    )
    total_keys = key_all.shape[0]
    block_rows = divisor_rows(total_keys, 1024)
    key_blocks = (
        key_all.reshape(total_keys // block_rows, block_rows, 2 * HD),
        slot_all.reshape(total_keys // block_rows, block_rows),
    )
    slot_column = slot_group[:, None]
    first_column = first_slot[:, None]

    def scores_of(key_block, slot_block):
        logits = (
            jnp.einsum("tqd,kd->tqk", queries, key_block, preferred_element_type=wide) * 0.125
        )
        allowed = (slot_block[None, :] <= slot_column) & (slot_block[None, :] >= first_column)
        return (logits, allowed[:, None, :])

    def absorb(running, blocks):
        running_max, running_sum, running_out = running
        key_block, slot_block = blocks
        logits, allowed = scores_of(key_block[:, :HD], slot_block)
        newest = jnp.maximum(running_max, jnp.max(jnp.where(allowed, logits, masked_fill), axis=-1))
        weights = jnp.where(allowed, jnp.exp(logits - newest[..., None]), 0.0)
        factor = jnp.exp(running_max - newest)
        running_sum = running_sum * factor + jnp.sum(weights, axis=-1)
        running_out = running_out * factor[..., None] + jnp.einsum(
            "tqk,kd->tqd", weights.astype(low), key_block[:, HD:], preferred_element_type=wide
        )
        return ((newest, running_sum, running_out), None)

    start_state = (
        jnp.full((rows, groups), masked_fill, wide),
        jnp.zeros((rows, groups), wide),
        jnp.zeros((rows, groups, HD), wide),
    )
    (final_max, final_sum, final_out), unused = lax.scan(absorb, start_state, key_blocks)
    attended = final_out / final_sum[..., None]
    log_total = final_max + jnp.log(final_sum)
    attended_low = attended.reshape(rows, query_width).astype(low)
    attended_low = after(attended_low, upstream_group)
    branch = first_sum(
        lambda first, end: jnp.dot(attended_low[first:end], out_w, preferred_element_type=wide),
        rows,
    )
    branch = other_sums(after(branch, gateup_here))
    branch = sub_sum(after(branch, *gateup_halves[0]))

    middle = inputs[:few] + branch
    scale_two = scale_of(middle)
    normed_two = middle * scale_two
    gu_w = jnp.concatenate(
        [piece.reshape(team_width, 2 * sub_units) for piece in gateup_pieces], axis=0
    )
    lowered_sub = sub_gather((normed_two * gains[1]).astype(low))
    lowered_group = heads_gather(after(lowered_sub, *gateup_halves[1]))
    hidden_grad = over_cols(upstream_group, down_w)
    gateup = jnp.dot(lowered_group, gu_w, preferred_element_type=wide)
    gate_pre = gateup[:, :sub_units]
    up_pre = gateup[:, sub_units:]
    sigmoid_gate = jax.nn.sigmoid(gate_pre)
    activated = gate_pre * sigmoid_gate
    hidden = (activated * up_pre).astype(low)
    gate_grad = hidden_grad * up_pre * sigmoid_gate * (1.0 + gate_pre * (1.0 - sigmoid_gate))
    up_grad = hidden_grad * activated
    gu_grad = jnp.concatenate([gate_grad, up_grad], axis=1).astype(low)
    lowered_grad_two = sub_sum(
        other_sums(first_sum(lambda first, end: over_cols(gu_grad[first:end], gu_w), rows))
    )
    gain_grad_two = jnp.sum(lowered_grad_two * normed_two, axis=0)
    middle_grad = upstream_share.astype(wide) + norm_back(
        scale_two, normed_two, lowered_grad_two * gains[1]
    )
    def team_cols(x, k):
        return x[:, k * team_width : (k + 1) * team_width]

    def gateup_term(k):
        return over_rows(team_cols(lowered_group, k), gu_grad).reshape(SUB, cols, 2 * sub_units)

    def down_term(k):
        term = over_rows(hidden, team_cols(upstream_group, k))
        return jnp.moveaxis(term.reshape(sub_units, SUB, cols), 1, 0)

    gateup_sum = teams_sum(gateup_term)
    down_sum = teams_sum(down_term)
    branch_sub = sub_gather(after(middle_grad.astype(low), gateup_sum))
    branch_grad = heads_gather(branch_sub)
    gateup_owned = sub_exchange(after(gateup_sum, branch_sub))
    down_owned = sub_exchange(after(down_sum, gateup_owned))
    mixed = sub_sum(
        other_sums(
            first_sum(
                lambda first, end: jnp.dot(
                    after(hidden, branch_grad)[first:end], down_w, preferred_element_type=wide
                ),
                rows,
            )
        )
    )
    block_out = teams_in_place((middle + mixed).astype(low))
    block_out = lax.all_gather(block_out, "heads", axis=0, tiled=True)

    attended_grad = over_cols(branch_grad, out_w).reshape(rows, groups, HD).astype(low)
    delta = jnp.sum(attended_grad.astype(wide) * attended, axis=-1)

    def backstep(query_grad, blocks):
        key_block, slot_block = blocks
        logits, allowed = scores_of(key_block[:, :HD], slot_block)
        probs = jnp.where(allowed, jnp.exp(logits - log_total[..., None]), 0.0)
        value_grad = jnp.einsum(
            "tqk,tqd->kd", probs.astype(low), attended_grad, preferred_element_type=wide
        )
        prob_grad = jnp.einsum(
            "tqd,kd->tqk", attended_grad, key_block[:, HD:], preferred_element_type=wide
        )
        score_grad = (probs * (prob_grad - delta[..., None])).astype(low)
        query_grad = query_grad + 0.125 * jnp.einsum(
            "tqk,kd->tqd", score_grad, key_block[:, :HD], preferred_element_type=wide
        )
        key_grad = 0.125 * jnp.einsum(
            "tqk,tqd->kd", score_grad, queries, preferred_element_type=wide
        )
        return (query_grad, jnp.concatenate([key_grad, value_grad], axis=-1))

    query_grad, keyval_terms = lax.scan(
        backstep, jnp.zeros((rows, groups, HD), wide), key_blocks
    )
    keyval_terms = keyval_terms.reshape(teams, rows, 2 * HD)
    keyval_sum = keyval_terms[0]
    for k in range(1, teams):
        keyval_sum = keyval_sum + swap(keyval_terms[k].astype(low), "fsdp", k).astype(wide)
    key_unrotated = rotate(keyval_sum[:, :HD], cosine_table, -sine_table)
    query_unrotated = rotate(query_grad, cosine_table, -sine_table).reshape(rows, query_width)
    qkv_grad = jnp.concatenate(
        [query_unrotated, key_unrotated, keyval_sum[:, HD:]], axis=-1
    ).astype(low)
    qkv_grad = after(qkv_grad, gateup_owned, down_sum)
    half_grad_one = first_sum(lambda first, end: over_cols(qkv_grad[first:end], qkv_w), rows)
    lowered_grad_one = sub_sum(after(other_sums(half_grad_one), down_owned))
    input_grad = middle_grad + norm_back(
        scale_one[:few], normed_one[:few], lowered_grad_one * gains[0]
    )
    input_grad = after(teams_in_place(input_grad.astype(low)), block_out)
    input_grad = lax.all_gather(input_grad, "heads", axis=0, tiled=True).astype(wide)

    def attention_term(k):
        late_grad = after(qkv_grad, half_grad_one) if k == 0 else qkv_grad
        qkv_term = over_rows(team_cols(lowered_one, k), late_grad)
        gain_term = jnp.sum(
            qkv_term * qkv_w[k * team_width : (k + 1) * team_width].astype(wide), axis=1
        ).reshape(SUB, 1, cols)
        gain_two_term = gain_grad_two[k * team_width : (k + 1) * team_width].reshape(SUB, 1, cols)
        gain_terms = jnp.concatenate([gain_term, gain_two_term], axis=1)
        out_term = over_rows(attended_low, team_cols(branch_grad, k))
        out_term = jnp.moveaxis(out_term.reshape(query_width, SUB, cols), 1, 0)
        return jnp.concatenate(
            [
                wider(qkv_term.reshape(SUB, cols, qkv_width), lanes, 2),
                wider(out_term, lanes, 2),
                wider(wider(gain_terms, lanes, 2), 16, 1),
            ],
            axis=1,
        )

    attention_owned = sub_exchange(after(teams_sum(attention_term), down_owned)).astype(wide)
    query_owned = jnp.concatenate(
        [attention_owned[k, :cols, :query_width] for k in range(SUB)], axis=1
    )[:, None]
    keyval_owned = jnp.sum(attention_owned[:, :cols, query_width:qkv_width], axis=0)[:, None]
    out_owned = attention_owned[:, cols : cols + query_width, :cols].reshape(
        1, SUB * query_width, cols
    )
    gains_owned = jnp.sum(
        attention_owned[:, cols + query_width : cols + query_width + 2, :cols], axis=0
    )
    for distance in heads_distances():
        gains_owned = gains_owned + swap(gains_owned, "heads", distance)
    gains_owned = jnp.stack([gains_owned[0] / norm_gains[0].astype(wide), gains_owned[1]], axis=0)
    gateup_owned = jnp.stack(
        [
            jnp.concatenate(
                [gateup_owned[k, :cols, c * sub_units : (c + 1) * sub_units] for k in range(SUB)],
                axis=1,
            )[:, :units]
            for c in range(2)
        ],
        axis=1,
    ).astype(wide)
    down_owned = down_owned.reshape(SUB * sub_units, cols)[:units].astype(wide)
    return (
        block_out,
        input_grad,
        gains_owned,
        query_owned,
        keyval_owned,
        out_owned,
        gateup_owned,
        down_owned,
    )


def solution(mesh):
    placed = (
        P("fsdp", None),
        P(None, "fsdp"),
        P("fsdp", "heads", None),
        P("fsdp", "heads", None),
        P("heads", None, "fsdp"),
        P("fsdp", None, "heads"),
        P("heads", "fsdp"),
        P(),
        P("fsdp"),
        P("fsdp", None),
    )
    return jax.shard_map(
        on_device,
        mesh=mesh,
        in_specs=placed,
        out_specs=(
            P("fsdp", None),
            P("fsdp", None),
            P(None, "fsdp"),
            P("fsdp", "heads", None),
            P("fsdp", "heads", None),
            P("heads", None, "fsdp"),
            P("fsdp", None, "heads"),
            P("heads", "fsdp"),
        ),
        check_vma=False,
    )
```

time: 496 us -> 442 us (0.89)
  local copies, waits for them, and re-layouts: 110 us -> 59.8 us
  between operations: 15.9 us -> 2.37 us
  matrix products: 43.7 us -> 53.1 us
  other arithmetic: 40.4 us -> 31.8 us
  starting transfers between devices: 93.9 us -> 99.4 us
  waiting for transfers between devices: 169 us -> 174 us
    ppermute x32 -> x51, waiting for transfers between devices: 31.6 us -> 137 us  [swap(): return lax.ppermute(x, axis, [(i, i ^ distance) for i in range(size)])]
    all_gather x2 -> x0, waiting for transfers between devices: 46.9 us -> none  [the longest x1 43.8 us: on_device(): out_w = lax.all_gather(w_out[0], 'fsdp', axis=1, tiled=True)]
    all_to_all x9 -> x0, waiting for transfers between devices: 44.6 us -> none  [the longest x5 30.5 us: to_all(): return lax.all_to_all(copies, axis, 0, 0, tiled=True)]
    all_to_all x9 -> x0, starting transfers between devices: 42.7 us -> none  [the longest x5 24.5 us: to_all(): return lax.all_to_all(copies, axis, 0, 0, tiled=True)]
    ppermute x32 -> x51, starting transfers between devices: 32 us -> 69 us  [swap(): return lax.ppermute(x, axis, [(i, i ^ distance) for i in range(size)])]
    concatenate x17 -> x3, local copies, waits for them, and re-layouts: 20.5 us -> 2.66 us  [heads_gather(): x = jnp.concatenate([x, swap(x, 'heads', distance)], axis=0)]
    all_to_all x4 -> x6, starting transfers between devices: 19.2 us -> 30.4 us  [sub_exchange(): return lax.all_to_all(x, 'fsdp', 0, 0, axis_index_groups=groups, tiled=True)]
    dot_general x13 -> x18, matrix products: 30.1 us -> 40.6 us  [the longest x8 19 us: over_rows(): lax.dot_general(left, right, (((0,), (0,)), ((), ())), preferred_element_...]
  transfers between devices with their start and end apart: 47 -> 57, of which waited for: 21 -> 31; matrix products, arithmetic and copies ran while one was open for 34% -> 28% of each run, Pallas kernels for 0% -> 0%
where the time goes in v2:
time: 442 us; the launch traced here: 436 us
  waiting for transfers between devices  174 us (39%)
  starting transfers between devices  99.4 us (22%)
  local copies, waits for them, and re-layouts  59.8 us (14%)
  matrix products  53.1 us (12%)
  other arithmetic  31.8 us (7%)
  blocking collectives  14.7 us (3%)
    ppermute x51, waiting for transfers between devices, swap(): return lax.ppermute(x, axis, [(i, i ^ distance) for i in range(size)])  137 us
    ppermute x51, starting transfers between devices, swap(): return lax.ppermute(x, axis, [(i, i ^ distance) for i in range(size)])  69 us
    all_to_all x6, waiting for transfers between devices, sub_exchange(): return lax.all_to_all(x, 'fsdp', 0, 0, axis_index_groups=groups, tiled=True)  37.6 us
    unnamed x158, local copies, waits for them, and re-layouts  32.1 us
    all_to_all x6, starting transfers between devices, sub_exchange(): return lax.all_to_all(x, 'fsdp', 0, 0, axis_index_groups=groups, tiled=True)  30.4 us
    dot_general x8, matrix products, over_rows(): lax.dot_general(left, right, (((0,), (0,)), ((), ())), preferred_element_...  19 us
    dot_general x6, matrix products, over_cols(): lax.dot_general(left, right, (((1,), (1,)), ((), ())), preferred_element_...  14.9 us
  transfers between devices with their start and end apart: 57, of which 31 were waited for; matrix products, arithmetic and copies ran while one was open for 28% of the time, Pallas kernels for 0%

profile of v2, /device:TPU:0, one launch (start us, length us, event | category | flops | bytes accessed | tf_op | source)
XLA Modules:
  0.0 435.7 jit_solution(10788028552478553191)
XLA Ops:
  12.3 5.1 %all-to-all-start = ((bf16[4,272,256]{2,1,0:T(8,128)(2,1)}), bf16[4,272,256]{2,1,0:T(8,128)(2,1)S(1)}, u32[]{:S(2)}, u32[]{:S(2)}) async-start(bf16[4,272,256]{2,1,0:T(8,128)(2,1)} %pad_maximum_fusion.18), calls=%async_computation | async-start | bytes 1114112 | tf_op jit(solution)/shard_map/all_to_all | solution.py:148
  26.5 9.5 %collective-permute-start.6 = (bf16[32,2048]{1,0:T(8,128)(2,1)S(1)}, bf16[32,2048]{1,0:T(8,128)(2,1)S(1)}, u32[]{:S(2)}, u32[]{:S(2)}) collective-permute-start(bf16[32,2048]{1,0:T(8,128)(2,1)S(1)} %constant_dynamic-update-slice_fusion.10), channel_id=1, source_target_pairs={{0,8},{4,12},{8,0},{12,4},{16,24},{20,28},{24,16},{28,20},{1,9},{5... | collective-permute-start | bytes 393224 | tf_op jit(solution)/shard_map/ppermute | solution.py:67
  56.7 6.5 %all-to-all-start.1 = ((bf16[4,512,256]{2,1,0:T(8,128)(2,1)}), bf16[4,512,256]{2,1,0:T(8,128)(2,1)}, u32[]{:S(2)}, u32[]{:S(2)}) async-start(bf16[4,512,256]{2,1,0:T(8,128)(2,1)} %pad_maximum_fusion.4), calls=%async_computation.1 | async-start | bytes 2097152 | tf_op jit(solution)/shard_map/all_to_all | solution.py:148
  82.7 7.1 %all-to-all-done.1 = bf16[4,512,256]{2,1,0:T(8,128)(2,1)} async-done(((bf16[4,512,256]{2,1,0:T(8,128)(2,1)}), bf16[4,512,256]{2,1,0:T(8,128)(2,1)}, u32[]{:S(2)}, u32[]{:S(2)}) %all-to-all-start.1) | async-done | bytes 1048608 | tf_op jit(solution)/shard_map/all_to_all | solution.py:148
  96.3 4.6 %all-to-all-start.2 = ((bf16[4,256,768]{2,1,0:T(8,128)(2,1)}), bf16[4,256,768]{2,1,0:T(8,128)(2,1)}, u32[]{:S(2)}, u32[]{:S(2)}) async-start(bf16[4,256,768]{2,1,0:T(8,128)(2,1)} %pad_maximum_fusion.1), calls=%async_computation.2 | async-start | bytes 3145728 | tf_op jit(solution)/shard_map/all_to_all | solution.py:148
  104.3 13.6 %collective-permute-done.12 = bf16[4,512,256]{2,1,0:T(8,128)(2,1)} collective-permute-done((bf16[4,512,256]{2,1,0:T(8,128)(2,1)}, bf16[4,512,256]{2,1,0:T(8,128)(2,1)}, u32[]{:S(2)}, u32[]{:S(2)}) %collective-permute-start.12) | collective-permute-done | bytes 1048608 | tf_op jit(solution)/shard_map/ppermute | solution.py:67
  127.2 10.5 %all-to-all-done.2 = bf16[4,256,768]{2,1,0:T(8,128)(2,1)} async-done(((bf16[4,256,768]{2,1,0:T(8,128)(2,1)}), bf16[4,256,768]{2,1,0:T(8,128)(2,1)}, u32[]{:S(2)}, u32[]{:S(2)}) %all-to-all-start.2) | async-done | bytes 1572896 | tf_op jit(solution)/shard_map/all_to_all | solution.py:148
  144.3 7.6 %collective-permute-done.14 = bf16[128,2048]{1,0:T(8,128)(2,1)S(1)} collective-permute-done((bf16[128,2048]{1,0:T(8,128)(2,1)S(1)}, bf16[128,2048]{1,0:T(8,128)(2,1)S(1)}, u32[]{:S(2)}, u32[]{:S(2)}) %collective-permute-start.14) | collective-permute-done | bytes 524320 | tf_op jit(solution)/shard_map/ppermute | solution.py:67
  152.0 8.5 %collective-permute-done.15 = bf16[2,256,768]{2,1,0:T(8,128)(2,1)S(1)} collective-permute-done((bf16[2,256,768]{2,1,0:T(8,128)(2,1)S(1)}, bf16[2,256,768]{2,1,0:T(8,128)(2,1)S(1)}, u32[]{:S(2)}, u32[]{:S(2)}) %collective-permute-start.15) | collective-permute-done | bytes 786464 | tf_op jit(solution)/shard_map/ppermute | solution.py:67
  187.1 10.7 %collective-permute-done.23 = bf16[128,2048]{1,0:T(8,128)(2,1)S(1)} collective-permute-done((bf16[128,2048]{1,0:T(8,128)(2,1)S(1)}, bf16[128,2048]{1,0:T(8,128)(2,1)S(1)}, u32[]{:S(2)}, u32[]{:S(2)}) %collective-permute-start.23) | collective-permute-done | bytes 524320 | tf_op jit(solution)/shard_map/ppermute | solution.py:67
  214.9 12.6 %collective-permute-done.26 = bf16[128,2048]{1,0:T(8,128)(2,1)S(1)} collective-permute-done((bf16[128,2048]{1,0:T(8,128)(2,1)S(1)}, bf16[128,2048]{1,0:T(8,128)(2,1)S(1)}, u32[]{:S(2)}, u32[]{:S(2)}) %collective-permute-start.26) | collective-permute-done | bytes 524320 | tf_op jit(solution)/shard_map/ppermute | solution.py:67
  232.2 14.0 %collective-permute-done.30 = bf16[4,256,768]{2,1,0:T(8,128)(2,1)S(1)} collective-permute-done((bf16[4,256,768]{2,1,0:T(8,128)(2,1)S(1)}, bf16[4,256,768]{2,1,0:T(8,128)(2,1)S(1)}, u32[]{:S(2)}, u32[]{:S(2)}) %collective-permute-start.30) | collective-permute-done | bytes 1572896 | tf_op jit(solution)/shard_map/ppermute | solution.py:67
  255.8 5.4 %collective-permute-done.32 = bf16[32,2048]{1,0:T(8,128)(2,1)S(1)} collective-permute-done((bf16[32,2048]{1,0:T(8,128)(2,1)S(1)}, bf16[32,2048]{1,0:T(8,128)(2,1)S(1)}, u32[]{:S(2)}, u32[]{:S(2)}) %collective-permute-start.32) | collective-permute-done | bytes 131104 | tf_op jit(solution)/shard_map/ppermute | solution.py:67
  264.2 7.9 %collective-permute-done.34 = bf16[128,2048]{1,0:T(8,128)(2,1)S(1)} collective-permute-done((bf16[128,2048]{1,0:T(8,128)(2,1)S(1)}, bf16[128,2048]{1,0:T(8,128)(2,1)S(1)}, u32[]{:S(2)}, u32[]{:S(2)}) %collective-permute-start.34) | collective-permute-done | bytes 524320 | tf_op jit(solution)/shard_map/ppermute | solution.py:67
  274.3 11.8 %fusion.27 = f32[384,1024]{1,0:T(8,128)S(1)} fusion(bf16[512,384]{1,0:T(8,128)(2,1)S(1)} %get-tuple-element.98, bf16[512,2048]{1,0:T(8,128)(2,1)S(1)} %copy-done.27), kind=kOutput, calls=%fused_computation.54 | convolution fusion | flops 402653184 | bytes 3014656 | tf_op jit(solution)/shard_map/dot_general | solution.py:201
  288.5 5.9 %all-to-all-start.3 = ((bf16[4,256,768]{2,1,0:T(8,128)(2,1)}), bf16[4,256,768]{2,1,0:T(8,128)(2,1)S(1)}, u32[]{:S(2)}, u32[]{:S(2)}) async-start(bf16[4,256,768]{2,1,0:T(8,128)(2,1)} %add_convert_fusion), calls=%async_computation.3 | async-start | bytes 3145728 | tf_op jit(solution)/shard_map/all_to_all | solution.py:148
  310.7 20.0 %all-to-all-done.3 = bf16[4,256,768]{2,1,0:T(8,128)(2,1)S(1)} async-done(((bf16[4,256,768]{2,1,0:T(8,128)(2,1)}), bf16[4,256,768]{2,1,0:T(8,128)(2,1)S(1)}, u32[]{:S(2)}, u32[]{:S(2)}) %all-to-all-start.3) | async-done | bytes 1572896 | tf_op jit(solution)/shard_map/all_to_all | solution.py:148
  333.4 4.2 all-to-all-start.4
  351.6 10.0 %collective-permute-done.37 = bf16[128,2048]{1,0:T(8,128)(2,1)S(1)} collective-permute-done((bf16[128,2048]{1,0:T(8,128)(2,1)S(1)}, bf16[128,2048]{1,0:T(8,128)(2,1)S(1)}, u32[]{:S(2)}, u32[]{:S(2)}) %collective-permute-start.37) | collective-permute-done | bytes 524320 | tf_op jit(solution)/shard_map/ppermute | solution.py:67
  376.8 6.8 %collective-permute-done.44 = bf16[128,2048]{1,0:T(8,128)(2,1)S(1)} collective-permute-done((bf16[128,2048]{1,0:T(8,128)(2,1)S(1)}, bf16[128,2048]{1,0:T(8,128)(2,1)S(1)}, u32[]{:S(2)}, u32[]{:S(2)}) %collective-permute-start.44) | collective-permute-done | bytes 524320 | tf_op jit(solution)/shard_map/ppermute | solution.py:67
  391.8 6.6 %collective-permute-done.47 = bf16[32,2048]{1,0:T(8,128)(2,1)S(1)} collective-permute-done((bf16[32,2048]{1,0:T(8,128)(2,1)S(1)}, bf16[32,2048]{1,0:T(8,128)(2,1)S(1)}, u32[]{:S(2)}, u32[]{:S(2)}) %collective-permute-start.47) | collective-permute-done | bytes 131104 | tf_op jit(solution)/shard_map/ppermute | solution.py:67
  398.5 7.9 %collective-permute-start.38 = (bf16[32,2048]{1,0:T(8,128)(2,1)S(1)}, bf16[32,2048]{1,0:T(8,128)(2,1)S(1)}, u32[]{:S(2)}, u32[]{:S(2)}) collective-permute-start(bf16[32,2048]{1,0:T(8,128)(2,1)S(1)} %copy-done.42), channel_id=1, source_target_pairs={{0,8},{4,12},{8,0},{12,4},{16,24},{20,28},{24,16},{28,20},{1,9},{5... | collective-permute-start | bytes 393224 | tf_op jit(solution)/shard_map/ppermute | solution.py:67
  411.9 7.4 %all_gather.6 = bf16[128,2048]{1,0:T(8,128)(2,1)S(1)} all-gather(bf16[32,2048]{1,0:T(8,128)(2,1)S(1)} %reshape.1830), channel_id=1, replica_groups=mesh['fsdp'=8,'heads'=4] {'heads'}, dimensions={0}, use_global_device_ids=true | all-gather | bytes 655360 | tf_op jit(solution)/shard_map/all_gather | solution.py:450
  419.8 7.3 %all_gather.7 = bf16[128,2048]{1,0:T(8,128)(2,1)S(1)} all-gather(bf16[32,2048]{1,0:T(8,128)(2,1)S(1)} %reshape.1834), channel_id=1, replica_groups=mesh['fsdp'=8,'heads'=4] {'heads'}, dimensions={0}, use_global_device_ids=true | all-gather | bytes 655360 | tf_op jit(solution)/shard_map/all_gather | solution.py:493
  (423 shorter events, 221.6 us)
Async XLA Ops:
  5.5 15.9 %collective-permute-start = (bf16[32,2048]{1,0:T(8,128)(2,1)}, bf16[32,2048]{1,0:T(8,128)(2,1)S(1)}, u32[]{:S(2)}, u32[]{:S(2)}) collective-permute-start(bf16[32,2048]{1,0:T(8,128)(2,1)} %get-tuple-element.240), channel_id=1, source_target_pairs={{0,8},{4,12},{8,0},{12,4},{16,24},{20,28},{24,16},{28,20},{1,9},{5... | collective-permute-start | bytes 393224 | tf_op jit(solution)/shard_map/ppermute | solution.py:67
  12.3 39.4 %all-to-all-start = ((bf16[4,272,256]{2,1,0:T(8,128)(2,1)}), bf16[4,272,256]{2,1,0:T(8,128)(2,1)S(1)}, u32[]{:S(2)}, u32[]{:S(2)}) async-start(bf16[4,272,256]{2,1,0:T(8,128)(2,1)} %pad_maximum_fusion.18), calls=%async_computation | async-start | bytes 1114112 | tf_op jit(solution)/shard_map/all_to_all | solution.py:148
  24.3 26.6 %collective-permute-start.3 = (bf16[128,2048]{1,0:T(8,128)(2,1)S(1)}, bf16[128,2048]{1,0:T(8,128)(2,1)S(1)}, u32[]{:S(2)}, u32[]{:S(2)}) collective-permute-start(bf16[128,2048]{1,0:T(8,128)(2,1)S(1)} %pad_maximum_fusion.19), channel_id=1, source_target_pairs={{0,2},{1,3},{2,0},{3,1},{4,6},{5,7},{6,4},{7,5},{8,10},{9,11},{10,... | collective-permute-start | bytes 1572872 | tf_op jit(solution)/shard_map/ppermute | solution.py:67
  56.7 33.1 %all-to-all-start.1 = ((bf16[4,512,256]{2,1,0:T(8,128)(2,1)}), bf16[4,512,256]{2,1,0:T(8,128)(2,1)}, u32[]{:S(2)}, u32[]{:S(2)}) async-start(bf16[4,512,256]{2,1,0:T(8,128)(2,1)} %pad_maximum_fusion.4), calls=%async_computation.1 | async-start | bytes 2097152 | tf_op jit(solution)/shard_map/all_to_all | solution.py:148
  92.8 25.1 %collective-permute-start.12 = (bf16[4,512,256]{2,1,0:T(8,128)(2,1)}, bf16[4,512,256]{2,1,0:T(8,128)(2,1)}, u32[]{:S(2)}, u32[]{:S(2)}) collective-permute-start(bf16[4,512,256]{2,1,0:T(8,128)(2,1)} %all-to-all-done.1), channel_id=1, source_target_pairs={{0,4},{4,0},{8,12},{12,8},{16,20},{20,16},{24,28},{28,24},{1,5},{5... | collective-permute-start | bytes 3145736 | tf_op jit(solution)/shard_map/ppermute | solution.py:67
  96.3 41.3 %all-to-all-start.2 = ((bf16[4,256,768]{2,1,0:T(8,128)(2,1)}), bf16[4,256,768]{2,1,0:T(8,128)(2,1)}, u32[]{:S(2)}, u32[]{:S(2)}) async-start(bf16[4,256,768]{2,1,0:T(8,128)(2,1)} %pad_maximum_fusion.1), calls=%async_computation.2 | async-start | bytes 3145728 | tf_op jit(solution)/shard_map/all_to_all | solution.py:148
  142.2 18.3 %collective-permute-start.15 = (bf16[2,256,768]{2,1,0:T(8,128)(2,1)S(1)}, bf16[2,256,768]{2,1,0:T(8,128)(2,1)S(1)}, u32[]{:S(2)}, u32[]{:S(2)}) collective-permute-start(bf16[2,256,768]{2,1,0:T(8,128)(2,1)S(1)} %get-tuple-element.169), channel_id=1, source_target_pairs={{0,4},{4,0},{8,12},{12,8},{16,20},{20,16},{24,28},{28,24},{1,5},{5... | collective-permute-start | bytes 2359304 | tf_op jit(solution)/shard_map/ppermute | solution.py:67
  166.0 17.9 %collective-permute-start.22 = (bf16[2,256,768]{2,1,0:T(8,128)(2,1)S(1)}, bf16[2,256,768]{2,1,0:T(8,128)(2,1)S(1)}, u32[]{:S(2)}, u32[]{:S(2)}) collective-permute-start(bf16[2,256,768]{2,1,0:T(8,128)(2,1)S(1)} %get-tuple-element.168), channel_id=1, source_target_pairs={{0,4},{4,0},{8,12},{12,8},{16,20},{20,16},{24,28},{28,24},{1,5},{5... | collective-permute-start | bytes 2359304 | tf_op jit(solution)/shard_map/ppermute | solution.py:67
  209.5 36.7 %collective-permute-start.30 = (bf16[4,256,768]{2,1,0:T(8,128)(2,1)S(1)}, bf16[4,256,768]{2,1,0:T(8,128)(2,1)S(1)}, u32[]{:S(2)}, u32[]{:S(2)}) collective-permute-start(bf16[4,256,768]{2,1,0:T(8,128)(2,1)S(1)} %bitcast.403), channel_id=1, source_target_pairs={{0,4},{4,0},{8,12},{12,8},{16,20},{20,16},{24,28},{28,24},{1,5},{5... | collective-permute-start | bytes 4718600 | tf_op jit(solution)/shard_map/ppermute | solution.py:67
  227.7 20.1 %collective-permute-start.29 = (bf16[32,2048]{1,0:T(8,128)(2,1)S(1)}, bf16[32,2048]{1,0:T(8,128)(2,1)S(1)}, u32[]{:S(2)}, u32[]{:S(2)}) collective-permute-start(bf16[32,2048]{1,0:T(8,128)(2,1)S(1)} %get-tuple-element.191), channel_id=1, source_target_pairs={{0,24},{4,28},{8,16},{12,20},{16,8},{20,12},{24,0},{28,4},{1,25},{... | collective-permute-start | bytes 393224 | tf_op jit(solution)/shard_map/ppermute | solution.py:67
  229.3 18.6 %collective-permute-start.28 = (bf16[32,2048]{1,0:T(8,128)(2,1)S(1)}, bf16[32,2048]{1,0:T(8,128)(2,1)S(1)}, u32[]{:S(2)}, u32[]{:S(2)}) collective-permute-start(bf16[32,2048]{1,0:T(8,128)(2,1)S(1)} %get-tuple-element.192), channel_id=1, source_target_pairs={{0,16},{4,20},{8,24},{12,28},{16,0},{20,4},{24,8},{28,12},{1,17},{... | collective-permute-start | bytes 393224 | tf_op jit(solution)/shard_map/ppermute | solution.py:67
  229.3 18.6 %collective-permute-start.27 = (bf16[32,2048]{1,0:T(8,128)(2,1)S(1)}, bf16[32,2048]{1,0:T(8,128)(2,1)S(1)}, u32[]{:S(2)}, u32[]{:S(2)}) collective-permute-start(bf16[32,2048]{1,0:T(8,128)(2,1)S(1)} %get-tuple-element.190), channel_id=1, source_target_pairs={{0,8},{4,12},{8,0},{12,4},{16,24},{20,28},{24,16},{28,20},{1,9},{5... | collective-permute-start | bytes 393224 | tf_op jit(solution)/shard_map/ppermute | solution.py:67
  263.6 22.6 %collective-permute-start.42 = (bf16[4,384,256]{2,1,0:T(8,128)(2,1)S(1)}, bf16[4,384,256]{2,1,0:T(8,128)(2,1)S(1)}, u32[]{:S(2)}, u32[]{:S(2)}) collective-permute-start(bf16[4,384,256]{2,1,0:T(8,128)(2,1)S(1)} %bitcast.370), channel_id=1, source_target_pairs={{0,4},{4,0},{8,12},{12,8},{16,20},{20,16},{24,28},{28,24},{1,5},{5... | collective-permute-start | bytes 2359304 | tf_op jit(solution)/shard_map/ppermute | solution.py:67
  273.0 21.4 %collective-permute-start.35 = (bf16[256,2048]{1,0:T(8,128)(2,1)}, bf16[256,2048]{1,0:T(8,128)(2,1)}, u32[]{:S(2)}, u32[]{:S(2)}) collective-permute-start(bf16[256,2048]{1,0:T(8,128)(2,1)} %get-tuple-element.188), channel_id=1, source_target_pairs={{0,1},{1,0},{2,3},{3,2},{4,5},{5,4},{6,7},{7,6},{8,9},{9,8},{10,11... | collective-permute-start | bytes 3145736 | tf_op jit(solution)/shard_map/ppermute | solution.py:67
  288.5 42.2 %all-to-all-start.3 = ((bf16[4,256,768]{2,1,0:T(8,128)(2,1)}), bf16[4,256,768]{2,1,0:T(8,128)(2,1)S(1)}, u32[]{:S(2)}, u32[]{:S(2)}) async-start(bf16[4,256,768]{2,1,0:T(8,128)(2,1)} %add_convert_fusion), calls=%async_computation.3 | async-start | bytes 3145728 | tf_op jit(solution)/shard_map/all_to_all | solution.py:148
  306.4 38.6 %collective-permute-start.36 = (bf16[256,2048]{1,0:T(8,128)(2,1)}, bf16[256,2048]{1,0:T(8,128)(2,1)}, u32[]{:S(2)}, u32[]{:S(2)}) collective-permute-start(bf16[256,2048]{1,0:T(8,128)(2,1)} %convolution_convert_fusion), channel_id=1, source_target_pairs={{0,1},{1,0},{2,3},{3,2},{4,5},{5,4},{6,7},{7,6},{8,9},{9,8},{10,11... | collective-permute-start | bytes 3145736 | tf_op jit(solution)/shard_map/ppermute | solution.py:67
  333.4 32.5 %collective-permute-start.43 = (bf16[256,2048]{1,0:T(8,128)(2,1)}, bf16[256,2048]{1,0:T(8,128)(2,1)}, u32[]{:S(2)}, u32[]{:S(2)}) collective-permute-start(bf16[256,2048]{1,0:T(8,128)(2,1)} %convolution_convert_fusion.2), channel_id=1, source_target_pairs={{0,1},{1,0},{2,3},{3,2},{4,5},{5,4},{6,7},{7,6},{8,9},{9,8},{10,11... | collective-permute-start | bytes 3145736 | tf_op jit(solution)/shard_map/ppermute | solution.py:67
  333.4 39.3 %all-to-all-start.4 = ((bf16[4,384,256]{2,1,0:T(8,128)(2,1)}), bf16[4,384,256]{2,1,0:T(8,128)(2,1)}, u32[]{:S(2)}, u32[]{:S(2)}) async-start(bf16[4,384,256]{2,1,0:T(8,128)(2,1)} %fusion.12), calls=%async_computation.4 | async-start | bytes 1572864 | tf_op jit(solution)/shard_map/all_to_all | solution.py:148
  344.2 27.4 %collective-permute-start.48 = (bf16[4,400,256]{2,1,0:T(8,128)(2,1)S(1)}, bf16[4,400,256]{2,1,0:T(8,128)(2,1)S(1)}, u32[]{:S(2)}, u32[]{:S(2)}) collective-permute-start(bf16[4,400,256]{2,1,0:T(8,128)(2,1)S(1)} %fusion.38), channel_id=1, source_target_pairs={{0,4},{4,0},{8,12},{12,8},{16,20},{20,16},{24,28},{28,24},{1,5},{5... | collective-permute-start | bytes 2457608 | tf_op jit(solution)/shard_map/ppermute | solution.py:67
  362.5 46.4 %collective-permute-start.40 = (bf16[32,2048]{1,0:T(8,128)(2,1)}, bf16[32,2048]{1,0:T(8,128)(2,1)}, u32[]{:S(2)}, u32[]{:S(2)}) collective-permute-start(bf16[32,2048]{1,0:T(8,128)(2,1)} %get-tuple-element.186), channel_id=1, source_target_pairs={{0,24},{4,28},{8,16},{12,20},{16,8},{20,12},{24,0},{28,4},{1,25},{... | collective-permute-start | bytes 393224 | tf_op jit(solution)/shard_map/ppermute | solution.py:67
  366.0 42.9 %collective-permute-start.39 = (bf16[32,2048]{1,0:T(8,128)(2,1)}, bf16[32,2048]{1,0:T(8,128)(2,1)}, u32[]{:S(2)}, u32[]{:S(2)}) collective-permute-start(bf16[32,2048]{1,0:T(8,128)(2,1)} %get-tuple-element.187), channel_id=1, source_target_pairs={{0,16},{4,20},{8,24},{12,28},{16,0},{20,4},{24,8},{28,12},{1,17},{... | collective-permute-start | bytes 393224 | tf_op jit(solution)/shard_map/ppermute | solution.py:67
  372.8 55.4 %all-to-all-start.5 = ((bf16[4,400,256]{2,1,0:T(8,128)(2,1)}), bf16[4,400,256]{2,1,0:T(8,128)(2,1)S(1)}, u32[]{:S(2)}, u32[]{:S(2)}) async-start(bf16[4,400,256]{2,1,0:T(8,128)(2,1)} %fusion.9), calls=%async_computation.5 | async-start | bytes 1638400 | tf_op jit(solution)/shard_map/all_to_all | solution.py:148
  386.7 21.0 %collective-permute-start.46 = (bf16[32,2048]{1,0:T(8,128)(2,1)S(1)}, bf16[32,2048]{1,0:T(8,128)(2,1)S(1)}, u32[]{:S(2)}, u32[]{:S(2)}) collective-permute-start(bf16[32,2048]{1,0:T(8,128)(2,1)S(1)} %get-tuple-element.184), channel_id=1, source_target_pairs={{0,16},{4,20},{8,24},{12,28},{16,0},{20,4},{24,8},{28,12},{1,17},{... | collective-permute-start | bytes 393224 | tf_op jit(solution)/shard_map/ppermute | solution.py:67
  387.7 20.0 %collective-permute-start.45 = (bf16[32,2048]{1,0:T(8,128)(2,1)S(1)}, bf16[32,2048]{1,0:T(8,128)(2,1)S(1)}, u32[]{:S(2)}, u32[]{:S(2)}) collective-permute-start(bf16[32,2048]{1,0:T(8,128)(2,1)S(1)} %get-tuple-element.182), channel_id=1, source_target_pairs={{0,8},{4,12},{8,0},{12,4},{16,24},{20,28},{24,16},{28,20},{1,9},{5... | collective-permute-start | bytes 393224 | tf_op jit(solution)/shard_map/ppermute | solution.py:67
  (94 other events, 980.7 us)
